TPU v7x, 256 devices: a whole 4x4x8 slice. The times are simulated.
256 devices in a mesh: tm: 64 (over y, x_lo, z), space: 4 (over x_hi, core).
Axes of the slice: x: 4 (x_hi: 2, x_lo: 2; x = x_hi * 2 + x_lo), y: 4, z: 8, core: 2. Of those that a mesh axis runs over, the one named last changes fastest.
Arguments:
- query: bfloat16 [512, 128, 1536], P('tm', 'space'), may hold values from -3 to 3
- key: bfloat16 [512, 128, 1536], P('tm', 'space'), may hold values from -3 to 3
- value: bfloat16 [512, 128, 1536], P('tm', 'space'), may hold values from -4 to 4
- grad_out: bfloat16 [512, 128, 1536], P('tm', 'space'), may hold values from -4 to 4
- group_order: int32 [128], replicated, may hold values from 0 to 127, as said below
- lookback: int32 [128], replicated, may hold values from 0 to 2, as said below
Outputs:
- grad_query: bfloat16 [512, 128, 1536], P('tm', 'space')
- grad_key: bfloat16 [512, 128, 1536], P('tm', 'space')
- grad_value: bfloat16 [512, 128, 1536], P('tm', 'space')
Inputs may be any that keep to these rules, and one draw needn't show every extreme that they name: `group_order`: slots 2i and 2i + 1 hold groups i and 127 - i, in either order, for every i below 64. `lookback`: some group of time index 2 or more has exactly 2.
All inputs are finite; a program needn't handle non-finite values.
Results may differ from a plain program's by a relative error of at most 0.005.
Values may be sent and summed in bfloat16 or wider, within the bound.
No kernel may reach another device: no remote copies, remote signals or barrier semaphores. Data moves between devices by JAX's collectives and lax.ppermute only.
A program may use at most 128 MiB of HBM per device.

v0:
```python
import functools

import jax
import jax.numpy as jnp
from jax import lax
from jax.experimental import pallas as pl
from jax.experimental.pallas import tpu as pltpu
from jax.sharding import PartitionSpec as P

HD = 64
LANES = 2 * HD
FACTOR = HD**-0.5
VMEM_LIMIT = 48 * 1024 * 1024
BF16 = jnp.bfloat16
F32 = jnp.float32


def params(**kwargs):
    return pltpu.CompilerParams(vmem_limit_bytes=VMEM_LIMIT, **kwargs)


def chain_swap(value, phase):
    count = lax.axis_size("tm")
    pairs = []
    for source in range(count):
        target = source ^ 1 if phase == 0 else ((source + 1) ^ 1) - 1
        if target == count:
            target = source
        if target >= 0:
            pairs.append((source, target))
    return lax.ppermute(value, "tm", pairs)


def space_swap(value, flip):
    count = lax.axis_size("space")
    return lax.ppermute(value, "space", [(i, i ^ flip) for i in range(count)])


def side_slots(order_ref):
    device = lax.axis_index("tm")
    early_slot = jnp.where(order_ref[2 * device] == device, 0, 1)
    odd = lax.rem(device, 2)
    slot0 = jnp.where(odd == 1, early_slot, 1 - early_slot)
    return slot0, 1 - slot0


def side_groups(entries):
    device = lax.axis_index("tm")
    odd = lax.rem(device, 2)
    late = entries - 1 - device
    return jnp.where(odd == 1, device, late), jnp.where(odd == 1, late, device)


def pack_chain_kernel(order_ref, key_ref, value_ref, out0_ref, out1_ref, sems):
    slot0, slot1 = side_slots(order_ref)
    frames, _, width = key_ref.shape
    half, cols = frames // 2, pl.ds(width // 2, width // 2)
    copies = []
    for index, (slot, out_ref) in enumerate(((slot1, out0_ref), (slot0, out1_ref))):
        for part, source in enumerate((key_ref, value_ref)):
            copies.append(
                pltpu.make_async_copy(
                    source.at[pl.ds(slot * half, half), :, cols],
                    out_ref.at[part],
                    sems.at[2 * index + part],
                )
            )
    for copy in copies:
        copy.start()
    for copy in copies:
        copy.wait()


def pack_chain(group_order, key, value):
    frames, patches, width = key.shape
    shape = jax.ShapeDtypeStruct((2, frames // 2, patches, width // 2), BF16)
    return pl.pallas_call(
        pack_chain_kernel,
        out_shape=(shape, shape),
        in_specs=[pl.BlockSpec(memory_space=pltpu.SMEM)] + [pl.BlockSpec(memory_space=pl.ANY)] * 2,
        out_specs=[pl.BlockSpec(memory_space=pl.ANY)] * 2,
        scratch_shapes=[pltpu.SemaphoreType.DMA((4,))],
        compiler_params=params(),
        name="pack_chain",
    )(group_order, key, value)


def pack_space_kernel(*refs):
    arrays, outs, sems = refs[:4], refs[4:7], refs[7]
    me = lax.axis_index("space")
    _, _, width = arrays[0].shape
    share = outs[0].shape[1]
    copies = []
    for index, out_ref in enumerate(outs):
        other = me ^ (index + 1)
        for part, source in enumerate(arrays):
            copies.append(
                pltpu.make_async_copy(
                    source.at[pl.ds(other * share, share), :, pl.ds(0, width // 2)],
                    out_ref.at[part],
                    sems.at[4 * index + part],
                )
            )
    for copy in copies:
        copy.start()
    for copy in copies:
        copy.wait()


def pack_space(query, key, value, grad):
    frames, patches, width = key.shape
    shape = jax.ShapeDtypeStruct((4, frames // 4, patches, width // 2), BF16)
    return pl.pallas_call(
        pack_space_kernel,
        out_shape=(shape,) * 3,
        in_specs=[pl.BlockSpec(memory_space=pl.ANY)] * 4,
        out_specs=[pl.BlockSpec(memory_space=pl.ANY)] * 3,
        scratch_shapes=[pltpu.SemaphoreType.DMA((12,))],
        compiler_params=params(),
        name="pack_space",
    )(query, key, value, grad)


def two_heads(rows):
    first = lax.broadcasted_iota(jnp.int32, rows.shape, 1) < HD
    zero = jnp.zeros_like(rows)
    return jnp.concatenate([jnp.where(first, rows, zero), jnp.where(first, zero, rows)], axis=0)


def rows_by_rows(left, right):
    return lax.dot_general(left, right, (((1,), (1,)), ((), ())), preferred_element_type=F32)


def attend(query, grad, blocks):
    scaled2 = two_heads(query * jnp.asarray(FACTOR, BF16))
    grad2 = two_heads(grad)
    unnormed, probs = [], []
    totals = weighted = None
    for key, value, weight in blocks:
        part = jnp.exp(rows_by_rows(key, scaled2))
        if weight is not None:
            part = part * weight
        grad_probs = rows_by_rows(value, grad2)
        total = jnp.sum(part, axis=0, keepdims=True)
        weigh = jnp.sum(part * grad_probs, axis=0, keepdims=True)
        totals = total if totals is None else totals + total
        weighted = weigh if weighted is None else weighted + weigh
        unnormed.append(part)
        probs.append(grad_probs)
    inverse = 1.0 / totals
    delta = weighted * inverse
    grad_query, grad_blocks = None, []
    for (key, _, _), part, grad_probs in zip(blocks, unnormed, probs):
        prob = part * inverse
        grad_scores = (prob * (grad_probs - delta)).astype(BF16)
        grad_value = jnp.dot(prob.astype(BF16), grad2, preferred_element_type=F32)
        grad_key = jnp.dot(grad_scores, scaled2, preferred_element_type=F32)
        piece = lax.dot_general(
            grad_scores, key, (((0,), (0,)), ((), ())), preferred_element_type=F32
        )
        grad_query = piece if grad_query is None else grad_query + piece
        grad_blocks.append((grad_key, grad_value))
    rows = query.shape[0]
    first = lax.broadcasted_iota(jnp.int32, (rows, LANES), 1) < HD
    grad_query = jnp.where(first, grad_query[:rows], grad_query[rows:]) * FACTOR
    return grad_query, grad_blocks


def chain_kernel(
    order_ref,
    lookback_ref,
    query_ref,
    key_ref,
    value_ref,
    grad_ref,
    near0_ref,
    near1_ref,
    far0_ref,
    far1_ref,
    dq_ref,
    own_ref,
    dnear0_ref,
    dnear1_ref,
    dfar0_ref,
    dfar1_ref,
):
    frames, patches, _ = query_ref.shape
    half = frames // 2
    rows = half * patches
    flat, tall = (rows, LANES), (half, patches, LANES)
    slots = side_slots(order_ref)
    groups = side_groups(order_ref.shape[0])
    key_patch = lax.rem(lax.broadcasted_iota(jnp.int32, (rows, 2 * rows), 0), patches)
    query_patch = lax.rem(lax.broadcasted_iota(jnp.int32, (rows, 2 * rows), 1), patches)
    same = (key_patch == query_patch).astype(F32)
    sides = ((near0_ref, far0_ref, dnear0_ref, dfar0_ref), (near1_ref, far1_ref, dnear1_ref, dfar1_ref))
    for slot, group, (near_ref, far_ref, dnear_ref, dfar_ref) in zip(slots, groups, sides):
        reach = jnp.minimum(lookback_ref[group], group)
        near_weight = same * jnp.where(reach >= 1, 1.0, 0.0)
        far_weight = same * jnp.where(reach >= 2, 1.0, 0.0)
        mine = pl.ds(slot * half, half)
        grad_query, ((dk, dv), (dk_near, dv_near), (dk_far, dv_far)) = attend(
            query_ref[mine].reshape(flat),
            grad_ref[mine].reshape(flat),
            (
                (key_ref[mine].reshape(flat), value_ref[mine].reshape(flat), same),
                (near_ref[0].reshape(flat), near_ref[1].reshape(flat), near_weight),
                (far_ref[0].reshape(flat), far_ref[1].reshape(flat), far_weight),
            ),
        )
        dq_ref[mine] = grad_query.astype(BF16).reshape(tall)
        own_ref[0, mine] = dk.reshape(tall)
        own_ref[1, mine] = dv.reshape(tall)
        dnear_ref[0] = dk_near.reshape(tall)
        dnear_ref[1] = dv_near.reshape(tall)
        dfar_ref[0] = dk_far.astype(BF16).reshape(tall)
        dfar_ref[1] = dv_far.astype(BF16).reshape(tall)


def chain_grads(group_order, lookback, query, key, value, grad, near0, near1, far0, far1):
    frames, patches, width = query.shape
    half, columns = frames // 2, width // 2
    steps = columns // LANES
    whole = pl.BlockSpec((frames, patches, LANES), lambda i, *_: (0, 0, steps + i))
    pair = pl.BlockSpec((2, half, patches, LANES), lambda i, *_: (0, 0, 0, i))
    pair_shape = (2, half, patches, columns)
    return pl.pallas_call(
        chain_kernel,
        grid_spec=pltpu.PrefetchScalarGridSpec(
            num_scalar_prefetch=2,
            grid=(steps,),
            in_specs=[whole] * 4 + [pair] * 4,
            out_specs=[
                pl.BlockSpec((frames, patches, LANES), lambda i, *_: (0, 0, i)),
                pl.BlockSpec((2, frames, patches, LANES), lambda i, *_: (0, 0, 0, i)),
            ]
            + [pair] * 4,
        ),
        out_shape=[
            jax.ShapeDtypeStruct((frames, patches, columns), BF16),
            jax.ShapeDtypeStruct((2, frames, patches, columns), F32),
            jax.ShapeDtypeStruct(pair_shape, F32),
            jax.ShapeDtypeStruct(pair_shape, F32),
            jax.ShapeDtypeStruct(pair_shape, BF16),
            jax.ShapeDtypeStruct(pair_shape, BF16),
        ],
        compiler_params=params(),
        cost_estimate=pl.CostEstimate(
            flops=800_000_000, bytes_accessed=8_000_000, transcendentals=1_200_000
        ),
        name="chain_grads",
    )(group_order, lookback, query, key, value, grad, near0, near1, far0, far1)


def space_kernel(
    query_ref, key_ref, value_ref, grad_ref, in1_ref, in2_ref, in3_ref, out0_ref, out1_ref, out2_ref, out3_ref
):
    me = lax.axis_index("space")
    share, patches = in1_ref.shape[1], in1_ref.shape[2]
    outs = (out0_ref, out1_ref, out2_ref, out3_ref)
    for frame in range(share):
        gathered = [
            jnp.concatenate(
                [own_ref[share * me + frame]] + [ref[part, frame] for ref in (in1_ref, in2_ref, in3_ref)],
                axis=0,
            )
            for part, own_ref in enumerate((query_ref, key_ref, value_ref, grad_ref))
        ]
        query, key, value, grad = gathered
        grad_query, ((grad_key, grad_value),) = attend(query, grad, ((key, value, None),))
        for part, result in enumerate((grad_query, grad_key, grad_value)):
            result = result.astype(BF16)
            for place, out_ref in enumerate(outs):
                out_ref[part, frame] = result[place * patches : (place + 1) * patches]


def space_grads(query, key, value, grad, arrived):
    frames, patches, width = query.shape
    share, columns = frames // 4, width // 2
    own = pl.BlockSpec((frames, patches, LANES), lambda i: (0, 0, i))
    return pl.pallas_call(
        space_kernel,
        grid=(columns // LANES,),
        in_specs=[own] * 4 + [pl.BlockSpec((4, share, patches, LANES), lambda i: (0, 0, 0, i))] * 3,
        out_specs=[pl.BlockSpec((3, share, patches, LANES), lambda i: (0, 0, 0, i))] * 4,
        out_shape=[jax.ShapeDtypeStruct((3, share, patches, columns), BF16)] * 4,
        compiler_params=params(),
        cost_estimate=pl.CostEstimate(
            flops=400_000_000, bytes_accessed=4_000_000, transcendentals=400_000
        ),
        name="space_grads",
    )(query, key, value, grad, *arrived)


def finish_kernel(steps, order_ref, *refs):
    parts, (dq_ref, own_ref, got0_ref, got1_ref), outs = refs[:4], refs[4:8], refs[8:]
    step = pl.program_id(0)
    share, frames = parts[0].shape[1], dq_ref.shape[0]
    half = frames // 2

    @pl.when(step < steps)
    def _():
        me = lax.axis_index("space")
        for flip, part_ref in enumerate(parts):
            place = pl.ds(share * (me ^ flip), share)
            for index, out_ref in enumerate(outs):
                out_ref[place] = part_ref[index]

    @pl.when(step >= steps)
    def _():
        outs[0][...] = dq_ref[...]
        for slot, got_ref in zip(side_slots(order_ref), (got0_ref, got1_ref)):
            mine = pl.ds(slot * half, half)
            for index in range(2):
                total = own_ref[index, mine] + got_ref[index].astype(F32)
                outs[1 + index][mine] = total.astype(BF16)


def finish(group_order, parts, dq, own, got0, got1):
    frames, patches, columns = dq.shape
    wide = 3 * LANES
    steps = columns // wide
    share = parts[0].shape[1]

    def early(i, *_):
        return (0, 0, 0, jnp.minimum(i, steps - 1))

    def late(i, *_):
        return (0, 0, 0, jnp.maximum(i - steps, 0))

    return pl.pallas_call(
        functools.partial(finish_kernel, steps),
        grid_spec=pltpu.PrefetchScalarGridSpec(
            num_scalar_prefetch=1,
            grid=(2 * steps,),
            in_specs=[pl.BlockSpec((3, share, patches, wide), early)] * 4
            + [
                pl.BlockSpec((frames, patches, wide), lambda i, *_: (0, 0, jnp.maximum(i - steps, 0))),
                pl.BlockSpec((2, frames, patches, wide), late),
                pl.BlockSpec((2, frames // 2, patches, wide), late),
                pl.BlockSpec((2, frames // 2, patches, wide), late),
            ],
            out_specs=[pl.BlockSpec((frames, patches, wide), lambda i, *_: (0, 0, i))] * 3,
        ),
        out_shape=[jax.ShapeDtypeStruct((frames, patches, 2 * columns), BF16)] * 3,
        compiler_params=params(),
        name="finish",
    )(group_order, *parts, dq, own, got0, got1)


def on_device(query, key, value, grad_out, group_order, lookback):
    chain0, chain1 = pack_chain(group_order, key, value)
    near0 = chain_swap(chain0, 0)
    near1 = chain_swap(chain1, 1)
    sent = pack_space(query, key, value, grad_out)
    arrived = [space_swap(part, flip) for flip, part in enumerate(sent, 1)]
    far1 = chain_swap(near0, 1)
    far0 = chain_swap(near1, 0)
    dq, own, dnear0, dnear1, dfar0, dfar1 = chain_grads(
        group_order, lookback, query, key, value, grad_out, near0, near1, far0, far1
    )
    back1 = chain_swap(dfar0, 0)
    back0 = chain_swap(dfar1, 1)
    results = space_grads(query, key, value, grad_out, arrived)
    parts = [results[0]] + [space_swap(part, flip) for flip, part in enumerate(results[1:], 1)]
    got0 = chain_swap((dnear1 + back1.astype(F32)).astype(BF16), 1)
    got1 = chain_swap((dnear0 + back0.astype(F32)).astype(BF16), 0)
    return tuple(finish(group_order, parts, dq, own, got0, got1))


def solution(mesh):
    spread = P("tm", "space", None)
    return jax.shard_map(
        on_device,
        mesh=mesh,
        in_specs=(spread,) * 4 + (P(), P()),
        out_specs=(spread,) * 3,
        check_vma=False,
    )
```

profile of v0, /device:TPU:1, one launch (start us, length us, event | category | flops | bytes accessed | tf_op | source)
XLA Modules:
  0.0 112.1 jit_solution(11634946879077412643)
XLA Ops:
  0.6 1.1 %copy-done = bf16[8,32,1536]{2,1,0:T(8,128)(2,1)S(1)} copy-done((bf16[8,32,1536]{2,1,0:T(8,128)(2,1)S(1)}, bf16[8,32,1536]{2,1,0:T(8,128)(2,1)}, u32[]{:S(2)}) %copy-start) | copy-done | bytes 786456
  1.8 1.1 %copy-done.2 = bf16[8,32,1536]{2,1,0:T(8,128)(2,1)S(1)} copy-done((bf16[8,32,1536]{2,1,0:T(8,128)(2,1)S(1)}, bf16[8,32,1536]{2,1,0:T(8,128)(2,1)}, u32[]{:S(2)}) %copy-start.2) | copy-done | bytes 786456
  2.9 0.7 copy-done.7
  3.6 0.7 pack_chain.1
  4.2 0.7 collective-permute-start.7
  4.9 0.0 copy-start.3
  4.9 0.0 copy-start.5
  5.0 5.4 %collective-permute-start.6 = (bf16[2,4,32,768]{3,2,1,0:T(8,128)(2,1)S(1)}, bf16[2,4,32,768]{3,2,1,0:T(8,128)(2,1)S(1)}, u32[]{:S(2)}, u32[]{:S(2)}) collective-permute-start(bf16[2,4,32,768]{3,2,1,0:T(8,128)(2,1)S(1)} %get-tuple-element.25), channel_id=1, source_target_pairs={{0,4},{4,0},{8,12},{12,8},{16,20},{20,16},{24,28},{28,24},{32,36},... | collective-permute-start | bytes 1179656 | tf_op jit(solution)/shard_map/ppermute | solution.py:31
  10.4 8.6 %collective-permute-start.8 = (bf16[2,4,32,768]{3,2,1,0:T(8,128)(2,1)S(1)}, bf16[2,4,32,768]{3,2,1,0:T(8,128)(2,1)S(1)}, u32[]{:S(2)}, u32[]{:S(2)}) collective-permute-start(bf16[2,4,32,768]{3,2,1,0:T(8,128)(2,1)S(1)} %collective-permute-done.7.near1_ref), channel_id=1, source_target_pairs={{0,4},{4,0},{8,12},{12,8},{16,20},{20,16},{24,28},{28,24},{32,36},... | collective-permute-start | bytes 1179656 | tf_op jit(solution)/shard_map/ppermute | solution.py:31
  19.0 0.7 collective-permute-start.9
  19.7 7.4 %collective-permute-done.8.far0_ref = bf16[2,4,32,768]{3,2,1,0:T(8,128)(2,1)S(1)} collective-permute-done((bf16[2,4,32,768]{3,2,1,0:T(8,128)(2,1)S(1)}, bf16[2,4,32,768]{3,2,1,0:T(8,128)(2,1)S(1)}, u32[]{:S(2)}, u32[]{:S(2)}) %collective-permute-start.8) | collective-permute-done | bytes 393248 | tf_op jit(solution)/shard_map/ppermute | solution.py:31
  27.1 9.5 %chain_grads.1 = (bf16[8,32,768]{2,1,0:T(8,128)(2,1)S(1)}, f32[2,8,32,768]{3,2,1,0:T(8,128)}, f32[2,4,32,768]{3,2,1,0:T(8,128)S(1)}, f32[2,4,32,768]{3,2,1,0:T(8...) custom-call(s32[128]{0:T(128)S(1)} %copy-done.7, s32[128]{0:T(128)S(1)} %copy-done.9, ...), custom_call_target="tpu_custom_call" | custom-call | flops 800000000 | bytes 8000000 | tf_op jit(solution)/shard_map/chain_grads/pallas_call | solution.py:227
  36.6 0.7 collective-permute-start.12
  37.3 8.6 %collective-permute-start.10 = (bf16[2,4,32,768]{3,2,1,0:T(8,128)(2,1)S(1)}, bf16[2,4,32,768]{3,2,1,0:T(8,128)(2,1)S(1)}, u32[]{:S(2)}, u32[]{:S(2)}) collective-permute-start(bf16[2,4,32,768]{3,2,1,0:T(8,128)(2,1)S(1)} %get-tuple-element.30), channel_id=1, source_target_pairs={{0,4},{4,0},{8,12},{12,8},{16,20},{20,16},{24,28},{28,24},{32,36},... | collective-permute-start | bytes 1179656 | tf_op jit(solution)/shard_map/ppermute | solution.py:31
  45.8 0.3 pack_space.1
  46.2 3.2 %collective-permute-start = (bf16[4,2,32,768]{3,2,1,0:T(8,128)(2,1)S(1)}, bf16[4,2,32,768]{3,2,1,0:T(8,128)(2,1)S(1)}, u32[]{:S(2)}, u32[]{:S(2)}) collective-permute-start(bf16[4,2,32,768]{3,2,1,0:T(8,128)(2,1)S(1)} %get-tuple-element.18), channel_id=1, source_target_pairs={{0,1},{1,0},{2,3},{3,2},{4,5},{5,4},{6,7},{7,6},{8,9},{9,8},{10,11... | collective-permute-start | bytes 1179656 | tf_op jit(solution)/shard_map/ppermute | solution.py:36
  49.3 2.8 %collective-permute-start.1 = (bf16[4,2,32,768]{3,2,1,0:T(8,128)(2,1)S(1)}, bf16[4,2,32,768]{3,2,1,0:T(8,128)(2,1)S(1)}, u32[]{:S(2)}, u32[]{:S(2)}) collective-permute-start(bf16[4,2,32,768]{3,2,1,0:T(8,128)(2,1)S(1)} %get-tuple-element.19), channel_id=1, source_target_pairs={{0,2},{1,3},{2,0},{3,1},{4,6},{5,7},{6,4},{7,5},{8,10},{9,11},{10,... | collective-permute-start | bytes 1179656 | tf_op jit(solution)/shard_map/ppermute | solution.py:36
  52.1 0.5 collective-permute-start.2
  52.6 0.1 add_convert_fusion
  52.7 0.4 collective-permute-start.13
  53.1 0.1 add_convert_fusion.1
  53.2 0.0 copy-start.8
  53.2 0.8 collective-permute-start.11
  54.0 24.6 %collective-permute-done.1.in2_ref = bf16[4,2,32,768]{3,2,1,0:T(8,128)(2,1)S(1)} collective-permute-done((bf16[4,2,32,768]{3,2,1,0:T(8,128)(2,1)S(1)}, bf16[4,2,32,768]{3,2,1,0:T(8,128)(2,1)S(1)}, u32[]{:S(2)}, u32[]{:S(2)}) %collective-permute-start.1) | collective-permute-done | bytes 393248 | tf_op jit(solution)/shard_map/ppermute | solution.py:36
  78.6 8.4 %collective-permute-done.2.in3_ref = bf16[4,2,32,768]{3,2,1,0:T(8,128)(2,1)S(1)} collective-permute-done((bf16[4,2,32,768]{3,2,1,0:T(8,128)(2,1)S(1)}, bf16[4,2,32,768]{3,2,1,0:T(8,128)(2,1)S(1)}, u32[]{:S(2)}, u32[]{:S(2)}) %collective-permute-start.2) | collective-permute-done | bytes 393248 | tf_op jit(solution)/shard_map/ppermute | solution.py:36
  87.0 5.0 %space_grads.1 = (bf16[3,2,32,768]{3,2,1,0:T(8,128)(2,1)S(1)}, bf16[3,2,32,768]{3,2,1,0:T(8,128)(2,1)S(1)}, bf16[3,2,32,768]{3,2,1,0:T(8,128)(2,1)S(1)}, bf16[3,2,32,768]{3,2,1,0:T(8,128)(2,1)S(1)}) custom-call(bf16[8,32,1536]{2,1,0:T(8,128)(2,1)S(1)} %copy-done.4, bf16[8,32,1536]{2,1,0:T(8,128)(2,1)S(1)} %copy-done.1, bf16[8,32,1536]{2,1,0:T(8,128)(2,1)S(1)} %copy-done.3, ...), custom_call_target="tpu_custom_call" | custom-call | flops 400000000 | bytes 4000000 | tf_op jit(solution)/shard_map/space_grads/pallas_call | solution.py:281
  92.0 0.5 collective-permute-start.3
  92.5 0.6 collective-permute-start.4
  93.1 2.7 %collective-permute-start.5 = (bf16[3,2,32,768]{3,2,1,0:T(8,128)(2,1)S(1)}, bf16[3,2,32,768]{3,2,1,0:T(8,128)(2,1)S(1)}, u32[]{:S(2)}, u32[]{:S(2)}) collective-permute-start(bf16[3,2,32,768]{3,2,1,0:T(8,128)(2,1)S(1)} %get-tuple-element.24), channel_id=1, source_target_pairs={{0,3},{1,2},{2,1},{3,0},{4,7},{5,6},{6,5},{7,4},{8,11},{9,10},{10,... | collective-permute-start | bytes 884744 | tf_op jit(solution)/shard_map/ppermute | solution.py:36
  95.8 6.7 %collective-permute-done.4.refs_2_ = bf16[3,2,32,768]{3,2,1,0:T(8,128)(2,1)S(1)} collective-permute-done((bf16[3,2,32,768]{3,2,1,0:T(8,128)(2,1)S(1)}, bf16[3,2,32,768]{3,2,1,0:T(8,128)(2,1)S(1)}, u32[]{:S(2)}, u32[]{:S(2)}) %collective-permute-start.4) | collective-permute-done | bytes 294944 | tf_op jit(solution)/shard_map/ppermute | solution.py:36
  102.5 6.6 %collective-permute-done.5.refs_3_ = bf16[3,2,32,768]{3,2,1,0:T(8,128)(2,1)S(1)} collective-permute-done((bf16[3,2,32,768]{3,2,1,0:T(8,128)(2,1)S(1)}, bf16[3,2,32,768]{3,2,1,0:T(8,128)(2,1)S(1)}, u32[]{:S(2)}, u32[]{:S(2)}) %collective-permute-start.5) | collective-permute-done | bytes 294944 | tf_op jit(solution)/shard_map/ppermute | solution.py:36
  109.1 3.0 %finish.1 = (bf16[8,32,1536]{2,1,0:T(8,128)(2,1)}, bf16[8,32,1536]{2,1,0:T(8,128)(2,1)}, bf16[8,32,1536]{2,1,0:T(8,128)(2,1)}) custom-call(s32[128]{0:T(128)S(1)} %copy-done.8, bf16[3,2,32,768]{3,2,1,0:T(8,128)(2,1)S(1)} %get-tuple-element.21.refs_0_, bf16[3,2,32,768]{3,2,1,0:T(8,128)(2,1)S(1)} %collective-permute-done.3.refs_1_, ...), custom_call_target="tpu_custom_call" | custom-call | tf_op jit(solution)/shard_map/finish/pallas_call | solution.py:331
  (23 shorter events, 0.1 us)
Async XLA Ops:
  0.6 1.1 %copy-start = (bf16[8,32,1536]{2,1,0:T(8,128)(2,1)S(1)}, bf16[8,32,1536]{2,1,0:T(8,128)(2,1)}, u32[]{:S(2)}) copy-start(bf16[8,32,1536]{2,1,0:T(8,128)(2,1)} %key_ref.5) | copy-start | bytes 2359300
  1.8 1.1 %copy-start.2 = (bf16[8,32,1536]{2,1,0:T(8,128)(2,1)S(1)}, bf16[8,32,1536]{2,1,0:T(8,128)(2,1)}, u32[]{:S(2)}) copy-start(bf16[8,32,1536]{2,1,0:T(8,128)(2,1)} %value_ref.5) | copy-start | bytes 2359300
  2.9 0.7 copy-start.7
  3.6 23.5 %copy-start.1 = (bf16[8,32,1536]{2,1,0:T(8,128)(2,1)S(1)}, bf16[8,32,1536]{2,1,0:T(8,128)(2,1)}, u32[]{:S(2)}) copy-start(bf16[8,32,1536]{2,1,0:T(8,128)(2,1)} %key_ref.5) | copy-start | bytes 2359300
  3.6 23.5 %copy-start.4 = (bf16[8,32,1536]{2,1,0:T(8,128)(2,1)S(1)}, bf16[8,32,1536]{2,1,0:T(8,128)(2,1)}, u32[]{:S(2)}) copy-start(bf16[8,32,1536]{2,1,0:T(8,128)(2,1)} %query_ref.3) | copy-start | bytes 2359300
  3.6 23.5 %copy-start.9 = (s32[128]{0:T(128)S(1)}, s32[128]{0:T(128)}, u32[]{:S(2)}) copy-start(s32[128]{0:T(128)} %lookback_ref.1) | copy-start | bytes 1540
  4.2 6.1 %collective-permute-start.7 = (bf16[2,4,32,768]{3,2,1,0:T(8,128)(2,1)S(1)}, bf16[2,4,32,768]{3,2,1,0:T(8,128)(2,1)S(1)}, u32[]{:S(2)}, u32[]{:S(2)}) collective-permute-start(bf16[2,4,32,768]{3,2,1,0:T(8,128)(2,1)S(1)} %get-tuple-element.26), channel_id=1, source_target_pairs={{4,8},{8,4},{12,16},{16,12},{20,24},{24,20},{28,32},{32,28},{36,40... | collective-permute-start | bytes 1179656 | tf_op jit(solution)/shard_map/ppermute | solution.py:31
  4.9 40.9 %copy-start.3 = (bf16[8,32,1536]{2,1,0:T(8,128)(2,1)S(1)}, bf16[8,32,1536]{2,1,0:T(8,128)(2,1)}, u32[]{:S(2)}) copy-start(bf16[8,32,1536]{2,1,0:T(8,128)(2,1)} %value_ref.5) | copy-start | bytes 2359300
  4.9 40.9 %copy-start.5 = (bf16[8,32,1536]{2,1,0:T(8,128)(2,1)S(1)}, bf16[8,32,1536]{2,1,0:T(8,128)(2,1)}, u32[]{:S(2)}) copy-start(bf16[8,32,1536]{2,1,0:T(8,128)(2,1)} %grad_ref.3) | copy-start | bytes 2359300
  5.0 14.0 %collective-permute-start.6 = (bf16[2,4,32,768]{3,2,1,0:T(8,128)(2,1)S(1)}, bf16[2,4,32,768]{3,2,1,0:T(8,128)(2,1)S(1)}, u32[]{:S(2)}, u32[]{:S(2)}) collective-permute-start(bf16[2,4,32,768]{3,2,1,0:T(8,128)(2,1)S(1)} %get-tuple-element.25), channel_id=1, source_target_pairs={{0,4},{4,0},{8,12},{12,8},{16,20},{20,16},{24,28},{28,24},{32,36},... | collective-permute-start | bytes 1179656 | tf_op jit(solution)/shard_map/ppermute | solution.py:31
  10.4 16.7 %collective-permute-start.8 = (bf16[2,4,32,768]{3,2,1,0:T(8,128)(2,1)S(1)}, bf16[2,4,32,768]{3,2,1,0:T(8,128)(2,1)S(1)}, u32[]{:S(2)}, u32[]{:S(2)}) collective-permute-start(bf16[2,4,32,768]{3,2,1,0:T(8,128)(2,1)S(1)} %collective-permute-done.7.near1_ref), channel_id=1, source_target_pairs={{0,4},{4,0},{8,12},{12,8},{16,20},{20,16},{24,28},{28,24},{32,36},... | collective-permute-start | bytes 1179656 | tf_op jit(solution)/shard_map/ppermute | solution.py:31
  19.0 8.1 %collective-permute-start.9 = (bf16[2,4,32,768]{3,2,1,0:T(8,128)(2,1)S(1)}, bf16[2,4,32,768]{3,2,1,0:T(8,128)(2,1)S(1)}, u32[]{:S(2)}, u32[]{:S(2)}) collective-permute-start(bf16[2,4,32,768]{3,2,1,0:T(8,128)(2,1)S(1)} %collective-permute-done.6.near0_ref), channel_id=1, source_target_pairs={{4,8},{8,4},{12,16},{16,12},{20,24},{24,20},{28,32},{32,28},{36,40... | collective-permute-start | bytes 1179656 | tf_op jit(solution)/shard_map/ppermute | solution.py:31
  36.6 16.0 %collective-permute-start.12 = (bf16[2,4,32,768]{3,2,1,0:T(8,128)(2,1)S(1)}, bf16[2,4,32,768]{3,2,1,0:T(8,128)(2,1)S(1)}, u32[]{:S(2)}, u32[]{:S(2)}) collective-permute-start(bf16[2,4,32,768]{3,2,1,0:T(8,128)(2,1)S(1)} %get-tuple-element.32), channel_id=1, source_target_pairs={{4,8},{8,4},{12,16},{16,12},{20,24},{24,20},{28,32},{32,28},{36,40... | collective-permute-start | bytes 1179656 | tf_op jit(solution)/shard_map/ppermute | solution.py:31
  37.3 15.8 %collective-permute-start.10 = (bf16[2,4,32,768]{3,2,1,0:T(8,128)(2,1)S(1)}, bf16[2,4,32,768]{3,2,1,0:T(8,128)(2,1)S(1)}, u32[]{:S(2)}, u32[]{:S(2)}) collective-permute-start(bf16[2,4,32,768]{3,2,1,0:T(8,128)(2,1)S(1)} %get-tuple-element.30), channel_id=1, source_target_pairs={{0,4},{4,0},{8,12},{12,8},{16,20},{20,16},{24,28},{28,24},{32,36},... | collective-permute-start | bytes 1179656 | tf_op jit(solution)/shard_map/ppermute | solution.py:31
  46.2 7.9 %collective-permute-start = (bf16[4,2,32,768]{3,2,1,0:T(8,128)(2,1)S(1)}, bf16[4,2,32,768]{3,2,1,0:T(8,128)(2,1)S(1)}, u32[]{:S(2)}, u32[]{:S(2)}) collective-permute-start(bf16[4,2,32,768]{3,2,1,0:T(8,128)(2,1)S(1)} %get-tuple-element.18), channel_id=1, source_target_pairs={{0,1},{1,0},{2,3},{3,2},{4,5},{5,4},{6,7},{7,6},{8,9},{9,8},{10,11... | collective-permute-start | bytes 1179656 | tf_op jit(solution)/shard_map/ppermute | solution.py:36
  49.3 29.3 %collective-permute-start.1 = (bf16[4,2,32,768]{3,2,1,0:T(8,128)(2,1)S(1)}, bf16[4,2,32,768]{3,2,1,0:T(8,128)(2,1)S(1)}, u32[]{:S(2)}, u32[]{:S(2)}) collective-permute-start(bf16[4,2,32,768]{3,2,1,0:T(8,128)(2,1)S(1)} %get-tuple-element.19), channel_id=1, source_target_pairs={{0,2},{1,3},{2,0},{3,1},{4,6},{5,7},{6,4},{7,5},{8,10},{9,11},{10,... | collective-permute-start | bytes 1179656 | tf_op jit(solution)/shard_map/ppermute | solution.py:36
  52.1 34.9 %collective-permute-start.2 = (bf16[4,2,32,768]{3,2,1,0:T(8,128)(2,1)S(1)}, bf16[4,2,32,768]{3,2,1,0:T(8,128)(2,1)S(1)}, u32[]{:S(2)}, u32[]{:S(2)}) collective-permute-start(bf16[4,2,32,768]{3,2,1,0:T(8,128)(2,1)S(1)} %get-tuple-element.20), channel_id=1, source_target_pairs={{0,3},{1,2},{2,1},{3,0},{4,7},{5,6},{6,5},{7,4},{8,11},{9,10},{10,... | collective-permute-start | bytes 1179656 | tf_op jit(solution)/shard_map/ppermute | solution.py:36
  52.7 56.4 %collective-permute-start.13 = (bf16[2,4,32,768]{3,2,1,0:T(8,128)(2,1)S(1)}, bf16[2,4,32,768]{3,2,1,0:T(8,128)(2,1)S(1)}, u32[]{:S(2)}, u32[]{:S(2)}) collective-permute-start(bf16[2,4,32,768]{3,2,1,0:T(8,128)(2,1)S(1)} %add_convert_fusion), channel_id=1, source_target_pairs={{0,4},{4,0},{8,12},{12,8},{16,20},{20,16},{24,28},{28,24},{32,36},... | collective-permute-start | bytes 1179656 | tf_op jit(solution)/shard_map/ppermute | solution.py:31
  53.2 55.9 %copy-start.6 = (f32[2,8,32,768]{3,2,1,0:T(8,128)S(1)}, f32[2,8,32,768]{3,2,1,0:T(8,128)}, u32[]{:S(2)}) copy-start(f32[2,8,32,768]{3,2,1,0:T(8,128)} %get-tuple-element.28.refs_5_) | copy-start | bytes 4718596
  53.2 55.9 %copy-start.8 = (s32[128]{0:T(128)S(1)}, s32[128]{0:T(128)}, u32[]{:S(2)}) copy-start(s32[128]{0:T(128)} %order_ref.5) | copy-start | bytes 1540
  53.2 55.9 %collective-permute-start.11 = (bf16[2,4,32,768]{3,2,1,0:T(8,128)(2,1)S(1)}, bf16[2,4,32,768]{3,2,1,0:T(8,128)(2,1)S(1)}, u32[]{:S(2)}, u32[]{:S(2)}) collective-permute-start(bf16[2,4,32,768]{3,2,1,0:T(8,128)(2,1)S(1)} %add_convert_fusion.1), channel_id=1, source_target_pairs={{4,8},{8,4},{12,16},{16,12},{20,24},{24,20},{28,32},{32,28},{36,40... | collective-permute-start | bytes 1179656 | tf_op jit(solution)/shard_map/ppermute | solution.py:31
  92.0 3.8 %collective-permute-start.3 = (bf16[3,2,32,768]{3,2,1,0:T(8,128)(2,1)S(1)}, bf16[3,2,32,768]{3,2,1,0:T(8,128)(2,1)S(1)}, u32[]{:S(2)}, u32[]{:S(2)}) collective-permute-start(bf16[3,2,32,768]{3,2,1,0:T(8,128)(2,1)S(1)} %get-tuple-element.22), channel_id=1, source_target_pairs={{0,1},{1,0},{2,3},{3,2},{4,5},{5,4},{6,7},{7,6},{8,9},{9,8},{10,11... | collective-permute-start | bytes 884744 | tf_op jit(solution)/shard_map/ppermute | solution.py:36
  92.5 10.0 %collective-permute-start.4 = (bf16[3,2,32,768]{3,2,1,0:T(8,128)(2,1)S(1)}, bf16[3,2,32,768]{3,2,1,0:T(8,128)(2,1)S(1)}, u32[]{:S(2)}, u32[]{:S(2)}) collective-permute-start(bf16[3,2,32,768]{3,2,1,0:T(8,128)(2,1)S(1)} %get-tuple-element.23), channel_id=1, source_target_pairs={{0,2},{1,3},{2,0},{3,1},{4,6},{5,7},{6,4},{7,5},{8,10},{9,11},{10,... | collective-permute-start | bytes 884744 | tf_op jit(solution)/shard_map/ppermute | solution.py:36
  93.1 16.0 %collective-permute-start.5 = (bf16[3,2,32,768]{3,2,1,0:T(8,128)(2,1)S(1)}, bf16[3,2,32,768]{3,2,1,0:T(8,128)(2,1)S(1)}, u32[]{:S(2)}, u32[]{:S(2)}) collective-permute-start(bf16[3,2,32,768]{3,2,1,0:T(8,128)(2,1)S(1)} %get-tuple-element.24), channel_id=1, source_target_pairs={{0,3},{1,2},{2,1},{3,0},{4,7},{5,6},{6,5},{7,4},{8,11},{9,10},{10,... | collective-permute-start | bytes 884744 | tf_op jit(solution)/shard_map/ppermute | solution.py:36
where the time goes:
time: 113 us; the launch traced here: 112 us
  waiting for transfers between devices  53.7 us (48%)
  starting transfers between devices  36 us (32%)
  Pallas kernels  18.5 us (16%)
  local copies, waits for them, and re-layouts  2.95 us (3%)
    ppermute x6, waiting for transfers between devices, space_swap(): return lax.ppermute(value, 'space', [(i, i ^ flip) for i in range(count)])  46.3 us
    ppermute x8, starting transfers between devices, chain_swap(): return lax.ppermute(value, 'tm', pairs)  25.8 us
    ppermute x6, starting transfers between devices, space_swap(): return lax.ppermute(value, 'space', [(i, i ^ flip) for i in range(count)])  10.2 us
    pallas_call x1, Pallas kernels, chain_grads(): pl.pallas_call(chain_kernel, grid_spec=pltpu.PrefetchScalarGridSpec(num_s...  9.49 us
    ppermute x8, waiting for transfers between devices, chain_swap(): return lax.ppermute(value, 'tm', pairs)  7.42 us
    pallas_call x1, Pallas kernels, space_grads(): pl.pallas_call(space_kernel, grid=(columns // LANES,), in_specs=[own] * 4...  5.01 us
    pallas_call x1, Pallas kernels, finish(): pl.pallas_call(functools.partial(finish_kernel, steps), grid_spec=pltpu.P...  3 us
    unnamed x20, local copies, waits for them, and re-layouts  2.95 us
  transfers between devices with their start and end apart: 14, of which 5 were waited for; matrix products, arithmetic and copies ran while one was open for 0% of the time, Pallas kernels for 5%

commit v1 on v0

v1 whole, which is shorter than its diff:
```python
import functools

import jax
import jax.numpy as jnp
from jax import lax
from jax.experimental import pallas as pl
from jax.experimental.pallas import tpu as pltpu
from jax.sharding import PartitionSpec as P

HD = 64
LANES = 2 * HD
CHAIN_LANES = 4 * HD
SPACE_LANES = 12 * HD
BAND = 16
FACTOR = HD**-0.5
VMEM_LIMIT = 48 * 1024 * 1024
BF16 = jnp.bfloat16
F32 = jnp.float32


def params(**kwargs):
    return pltpu.CompilerParams(vmem_limit_bytes=VMEM_LIMIT, **kwargs)


def chain_swap(value, phase):
    count = lax.axis_size("tm")
    pairs = []
    for source in range(count):
        target = source ^ 1 if phase == 0 else ((source + 1) ^ 1) - 1
        if target == count:
            target = source
        if target >= 0:
            pairs.append((source, target))
    return lax.ppermute(value, "tm", pairs)


def space_swap(value, flip):
    count = lax.axis_size("space")
    return lax.ppermute(value, "space", [(i, i ^ flip) for i in range(count)])


def side_slots(order_ref):
    device = lax.axis_index("tm")
    early_slot = jnp.where(order_ref[2 * device] == device, 0, 1)
    odd = lax.rem(device, 2)
    slot0 = jnp.where(odd == 1, early_slot, 1 - early_slot)
    return slot0, 1 - slot0


def side_groups(entries):
    device = lax.axis_index("tm")
    odd = lax.rem(device, 2)
    late = entries - 1 - device
    return jnp.where(odd == 1, device, late), jnp.where(odd == 1, late, device)


def pack_kernel(order_ref, query_ref, key_ref, value_ref, grad_ref, *refs):
    chain_refs, space_refs, sems = refs[:2], refs[2:5], refs[5]
    slot0, slot1 = side_slots(order_ref)
    me = lax.axis_index("space")
    frames, _, width = key_ref.shape
    half, share, columns = frames // 2, frames // 4, width // 2
    copies = []

    def send(source, first, count, column, target):
        piece = source.at[pl.ds(first, count), :, pl.ds(column, columns)]
        copies.append(pltpu.make_async_copy(piece, target, sems.at[len(copies)]))

    for here, there, out_ref in ((slot0, slot1, chain_refs[0]), (slot1, slot0, chain_refs[1])):
        send(key_ref, there * half, half, columns, out_ref.at[0])
        send(value_ref, there * half, half, columns, out_ref.at[1])
        send(query_ref, here * half, half, columns, out_ref.at[2])
        send(grad_ref, here * half, half, columns, out_ref.at[3])
    for flip, out_ref in enumerate(space_refs, 1):
        for part, source in enumerate((query_ref, key_ref, value_ref, grad_ref)):
            send(source, (me ^ flip) * share, share, 0, out_ref.at[part])
    for copy in copies:
        copy.start()
    for copy in copies:
        copy.wait()


def pack(group_order, query, key, value, grad):
    frames, patches, width = key.shape
    chain = jax.ShapeDtypeStruct((4, frames // 2, patches, width // 2), BF16)
    space = jax.ShapeDtypeStruct((4, frames // 4, patches, width // 2), BF16)
    outs = pl.pallas_call(
        pack_kernel,
        out_shape=(chain, chain, space, space, space),
        in_specs=[pl.BlockSpec(memory_space=pltpu.SMEM)] + [pl.BlockSpec(memory_space=pl.ANY)] * 4,
        out_specs=[pl.BlockSpec(memory_space=pl.ANY)] * 5,
        scratch_shapes=[pltpu.SemaphoreType.DMA((20,))],
        compiler_params=params(),
        name="pack",
    )(group_order, *[pltpu.with_memory_space_constraint(x, pltpu.HBM) for x in (query, key, value, grad)])
    return outs[:2], outs[2:]


def per_head(rows):
    head = lax.broadcasted_iota(jnp.int32, rows.shape, 1) // HD
    zero = jnp.zeros_like(rows)
    return jnp.concatenate([jnp.where(head == h, rows, zero) for h in range(rows.shape[1] // HD)], axis=0)


def own_head(bands):
    heads = bands.shape[1] // HD
    rows = bands.shape[0] // heads
    head = lax.broadcasted_iota(jnp.int32, (rows, bands.shape[1]), 1) // HD
    result = bands[:rows]
    for h in range(1, heads):
        result = jnp.where(head == h, bands[h * rows : (h + 1) * rows], result)
    return result


BY_ROWS = (((1,), (1,)), ((), ()))
BY_COLUMNS = (((0,), (0,)), ((), ()))


def pairs(key, value, scaled, grads, weight):
    unnormed = jnp.exp(lax.dot_general(key, scaled, BY_ROWS, preferred_element_type=F32))
    if weight is not None:
        unnormed = unnormed * weight
    return unnormed, lax.dot_general(value, grads, BY_ROWS, preferred_element_type=F32)


def sums(unnormed, grad_probs):
    return jnp.sum(unnormed, axis=0, keepdims=True), jnp.sum(unnormed * grad_probs, axis=0, keepdims=True)


def gradients(key, scaled, grads, unnormed, grad_probs, totals, weighted):
    inverse = jnp.where(totals > 0.0, 1.0 / totals, 0.0)
    prob = unnormed * inverse
    grad_scores = (prob * (grad_probs - weighted * inverse)).astype(BF16)
    grad_value = jnp.dot(prob.astype(BF16), grads, preferred_element_type=F32)
    grad_key = jnp.dot(grad_scores, scaled, preferred_element_type=F32)
    bands = lax.dot_general(grad_scores, key, BY_COLUMNS, preferred_element_type=F32)
    return own_head(bands) * FACTOR, grad_key, grad_value


def scale(query):
    return per_head(query * jnp.asarray(FACTOR, BF16))


def attend(query, key, value, grad):
    scaled, grads = scale(query), per_head(grad)
    unnormed, grad_probs = pairs(key, value, scaled, grads, None)
    return gradients(key, scaled, grads, unnormed, grad_probs, *sums(unnormed, grad_probs))


class Side:
    def __init__(self, side, order_ref, lookback_ref, locals_, before_ref, after_ref):
        self.locals, self.before, self.after = locals_, before_ref, after_ref
        frames, self.patches, self.lanes = locals_[0].shape
        self.half = frames // 2
        self.rows = self.half * BAND
        self.heads = self.lanes // HD
        self.mine = pl.ds(side_slots(order_ref)[side] * self.half, self.half)
        entries = order_ref.shape[0]
        group = side_groups(entries)[side]
        reach = jnp.minimum(lookback_ref[group], group)
        following = jnp.minimum(group + 1, entries - 1)
        reach_after = jnp.where(group + 1 < entries, jnp.minimum(lookback_ref[following], following), 0)
        shape = (2 * self.rows, self.heads * self.rows)
        key_row = lax.broadcasted_iota(jnp.int32, shape, 0)
        query_row = lax.broadcasted_iota(jnp.int32, shape, 1)
        same = lax.rem(key_row, BAND) == lax.rem(query_row, BAND)
        allowed = same & (key_row // self.rows <= reach)
        self.weight = jnp.where(allowed, 1.0, 0.0)
        self.skip_weight = jnp.where(same & (reach_after >= 2), 1.0, 0.0)[: self.rows]

    def flat(self, piece):
        return piece.reshape(self.rows, self.lanes)

    def load(self, band):
        at = pl.ds(band * BAND, BAND)
        query, key, value, grad = (self.flat(ref[self.mine, at]) for ref in self.locals)
        key_before, value_before = (self.flat(self.before[index, :, at]) for index in (0, 1))
        query_after, grad_after = (self.flat(self.after[index, :, at]) for index in (2, 3))
        keys = jnp.concatenate([key, key_before], axis=0)
        values = jnp.concatenate([value, value_before], axis=0)
        near = (keys, scale(query), per_head(grad))
        skip = (key_before, scale(query_after), per_head(grad_after))
        near_pairs = pairs(keys, values, near[1], near[2], self.weight)
        skip_pairs = pairs(key_before, value_before, skip[1], skip[2], self.skip_weight)
        return near + near_pairs, skip + skip_pairs


def both_sides(order_ref, lookback_ref, locals_, got0_ref, got1_ref):
    return (
        Side(0, order_ref, lookback_ref, locals_, got0_ref, got1_ref),
        Side(1, order_ref, lookback_ref, locals_, got1_ref, got0_ref),
    )


def chain_sums_kernel(
    order_ref, lookback_ref, query_ref, key_ref, value_ref, grad_ref, got0_ref, got1_ref, out0_ref, out1_ref
):
    sides = both_sides(order_ref, lookback_ref, (query_ref, key_ref, value_ref, grad_ref), got0_ref, got1_ref)
    for side, near_out, skip_out in zip(sides, (out0_ref, out1_ref), (out1_ref, out0_ref)):
        for band in range(side.patches // BAND):
            near, skip = side.load(band)
            near_out[0, band, 0:1], near_out[0, band, 1:2] = sums(*near[3:])
            skip_out[0, band, 2:3], skip_out[0, band, 3:4] = sums(*skip[3:])


def chain_grads_kernel(
    order_ref,
    lookback_ref,
    query_ref,
    key_ref,
    value_ref,
    grad_ref,
    got0_ref,
    got1_ref,
    sums0_ref,
    sums1_ref,
    from0_ref,
    from1_ref,
    own_ref,
    out0_ref,
    out1_ref,
):
    sides = both_sides(order_ref, lookback_ref, (query_ref, key_ref, value_ref, grad_ref), got0_ref, got1_ref)
    mine, others, outs = (sums0_ref, sums1_ref), (from0_ref, from1_ref), (out0_ref, out1_ref)
    for number, side in enumerate(sides):
        rows, tall = side.rows, (side.half, BAND, side.lanes)
        for band in range(side.patches // BAND):
            at = pl.ds(band * BAND, BAND)
            near, skip = side.load(band)

            def whole_sums(row):
                place = number if row == 0 else 1 - number
                ours, theirs = mine[place], others[place]
                return [
                    ours[0, band, row + k : row + k + 1] + theirs[0, band, 2 - row + k : 3 - row + k] for k in (0, 1)
                ]

            dq, dk, dv = gradients(*near, *whole_sums(0))
            dq_after, dk_before, dv_before = gradients(*skip, *whole_sums(2))
            own_ref[0, side.mine, at] = dq.reshape(tall)
            own_ref[1, side.mine, at] = dk[:rows].reshape(tall)
            own_ref[2, side.mine, at] = dv[:rows].reshape(tall)
            back, on = outs[number], outs[1 - number]
            back[0, :, at] = (dk[rows:] + dk_before).astype(BF16).reshape(tall)
            back[1, :, at] = (dv[rows:] + dv_before).astype(BF16).reshape(tall)
            on[2, :, at] = dq_after.astype(BF16).reshape(tall)


def chain_specs(query):
    frames, patches, width = query.shape
    half, columns = frames // 2, width // 2
    steps = columns // CHAIN_LANES
    bands = patches // BAND
    wide = CHAIN_LANES // HD * half * BAND
    whole = pl.BlockSpec((frames, patches, CHAIN_LANES), lambda i, *_: (0, 0, steps + i))
    got = pl.BlockSpec((4, half, patches, CHAIN_LANES), lambda i, *_: (0, 0, 0, i))
    part = pl.BlockSpec((1, bands, 4, wide), lambda i, *_: (i, 0, 0, 0))
    return steps, [whole] * 4 + [got] * 2, part, jax.ShapeDtypeStruct((steps, bands, 4, wide), F32)


def chain_sums(group_order, lookback, query, key, value, grad, got0, got1):
    steps, in_specs, part, shape = chain_specs(query)
    return pl.pallas_call(
        chain_sums_kernel,
        grid_spec=pltpu.PrefetchScalarGridSpec(
            num_scalar_prefetch=2, grid=(steps,), in_specs=in_specs, out_specs=[part] * 2
        ),
        out_shape=[shape] * 2,
        compiler_params=params(),
        name="chain_sums",
    )(group_order, lookback, query, key, value, grad, got0, got1)


def chain_grads(group_order, lookback, query, key, value, grad, got0, got1, ours, theirs):
    frames, patches, width = query.shape
    half, columns = frames // 2, width // 2
    steps, in_specs, part, _ = chain_specs(query)
    sent = jax.ShapeDtypeStruct((3, half, patches, columns), BF16)
    return pl.pallas_call(
        chain_grads_kernel,
        grid_spec=pltpu.PrefetchScalarGridSpec(
            num_scalar_prefetch=2,
            grid=(steps,),
            in_specs=in_specs + [part] * 4,
            out_specs=[pl.BlockSpec((3, frames, patches, CHAIN_LANES), lambda i, *_: (0, 0, 0, i))]
            + [pl.BlockSpec((3, half, patches, CHAIN_LANES), lambda i, *_: (0, 0, 0, i))] * 2,
        ),
        out_shape=[jax.ShapeDtypeStruct((3, frames, patches, columns), F32), sent, sent],
        compiler_params=params(),
        name="chain_grads",
    )(group_order, lookback, query, key, value, grad, got0, got1, *ours, *theirs)


def space_kernel(
    query_ref, key_ref, value_ref, grad_ref, in1_ref, in2_ref, in3_ref, out0_ref, out1_ref, out2_ref, out3_ref
):
    me = lax.axis_index("space")
    share, patches = in1_ref.shape[1], in1_ref.shape[2]
    outs = (out0_ref, out1_ref, out2_ref, out3_ref)
    for frame in range(share):
        gathered = [
            jnp.concatenate(
                [own_ref[share * me + frame]] + [ref[part, frame] for ref in (in1_ref, in2_ref, in3_ref)],
                axis=0,
            )
            for part, own_ref in enumerate((query_ref, key_ref, value_ref, grad_ref))
        ]
        couples = [
            attend(*(rows[:, c : c + LANES] for rows in gathered))
            for c in range(0, gathered[0].shape[1], LANES)
        ]
        grad_query, grad_key, grad_value = (jnp.concatenate(x, axis=1) for x in zip(*couples))
        for part, result in enumerate((grad_query, grad_key, grad_value)):
            result = result.astype(BF16)
            for place, out_ref in enumerate(outs):
                out_ref[part, frame] = result[place * patches : (place + 1) * patches]


def space_grads(query, key, value, grad, arrived):
    frames, patches, width = query.shape
    share, columns = frames // 4, width // 2
    own = pl.BlockSpec((frames, patches, SPACE_LANES), lambda i: (0, 0, i))
    return pl.pallas_call(
        space_kernel,
        grid=(columns // SPACE_LANES,),
        in_specs=[own] * 4 + [pl.BlockSpec((4, share, patches, SPACE_LANES), lambda i: (0, 0, 0, i))] * 3,
        out_specs=[pl.BlockSpec((3, share, patches, SPACE_LANES), lambda i: (0, 0, 0, i))] * 4,
        out_shape=[jax.ShapeDtypeStruct((3, share, patches, columns), BF16)] * 4,
        compiler_params=params(),
        cost_estimate=pl.CostEstimate(
            flops=400_000_000, bytes_accessed=4_000_000, transcendentals=400_000
        ),
        name="space_grads",
    )(query, key, value, grad, *arrived)


def finish_kernel(steps, order_ref, *refs):
    parts, (own_ref, got0_ref, got1_ref), outs = refs[:4], refs[4:7], refs[7:]
    step = pl.program_id(0)
    share, frames = parts[0].shape[1], own_ref.shape[1]
    half = frames // 2

    @pl.when(step < steps)
    def _():
        me = lax.axis_index("space")
        for flip, part_ref in enumerate(parts):
            place = pl.ds(share * (me ^ flip), share)
            for index, out_ref in enumerate(outs):
                out_ref[place] = part_ref[index]

    @pl.when(step >= steps)
    def _():
        slots = side_slots(order_ref)
        for slot, query_ref, key_ref in zip(slots, (got0_ref, got1_ref), (got1_ref, got0_ref)):
            mine = pl.ds(slot * half, half)
            arrived = (query_ref[2], key_ref[0], key_ref[1])
            for index, (out_ref, piece) in enumerate(zip(outs, arrived)):
                out_ref[mine] = (own_ref[index, mine] + piece.astype(F32)).astype(BF16)


def finish(group_order, parts, own, got0, got1):
    _, frames, patches, columns = own.shape
    wide = 3 * LANES
    steps = columns // wide
    share = parts[0].shape[1]

    def early(i, *_):
        return (0, 0, 0, jnp.minimum(i, steps - 1))

    def late(i, *_):
        return (0, 0, 0, jnp.maximum(i - steps, 0))

    return pl.pallas_call(
        functools.partial(finish_kernel, steps),
        grid_spec=pltpu.PrefetchScalarGridSpec(
            num_scalar_prefetch=1,
            grid=(2 * steps,),
            in_specs=[pl.BlockSpec((3, share, patches, wide), early)] * 4
            + [pl.BlockSpec((3, frames, patches, wide), late)]
            + [pl.BlockSpec((3, frames // 2, patches, wide), late)] * 2,
            out_specs=[pl.BlockSpec((frames, patches, wide), lambda i, *_: (0, 0, i))] * 3,
        ),
        out_shape=[jax.ShapeDtypeStruct((frames, patches, 2 * columns), BF16)] * 3,
        compiler_params=params(),
        name="finish",
    )(group_order, *parts, own, got0, got1)


def on_device(query, key, value, grad_out, group_order, lookback):
    chain, sent = pack(group_order, query, key, value, grad_out)
    sent = list(sent)
    got = [chain_swap(part, phase) for phase, part in enumerate(chain)]
    arrived = [space_swap(part, flip) for flip, part in enumerate(sent, 1)]
    ours = chain_sums(group_order, lookback, query, key, value, grad_out, *got)
    theirs = [chain_swap(part, phase) for phase, part in enumerate(ours)]
    own, *back = chain_grads(group_order, lookback, query, key, value, grad_out, *got, ours, theirs)
    back = [chain_swap(part, phase) for phase, part in enumerate(back)]
    results = space_grads(query, key, value, grad_out, arrived)
    parts = [results[0]] + [space_swap(part, flip) for flip, part in enumerate(results[1:], 1)]
    return tuple(finish(group_order, parts, own, *back))


def solution(mesh):
    spread = P("tm", "space", None)
    return jax.shard_map(
        on_device,
        mesh=mesh,
        in_specs=(spread,) * 4 + (P(), P()),
        out_specs=(spread,) * 3,
        check_vma=False,
    )
```

time: 113 us -> 85.1 us (0.75)
  waiting for transfers between devices: 53.7 us -> 38.3 us
  starting transfers between devices: 36 us -> 26.2 us
  local copies, waits for them, and re-layouts: 2.95 us -> 0.82 us
    ppermute x6, waiting for transfers between devices: 46.3 us -> 26.2 us  [space_swap(): return lax.ppermute(value, 'space', [(i, i ^ flip) for i in range(count)])]
    ppermute x8 -> x6, starting transfers between devices: 25.8 us -> 15.8 us  [chain_swap(): return lax.ppermute(value, 'tm', pairs)]
    ppermute x8 -> x6, waiting for transfers between devices: 7.42 us -> 12.1 us  [chain_swap(): return lax.ppermute(value, 'tm', pairs)]
    unnamed x20 -> x14, local copies, waits for them, and re-layouts: 2.95 us -> 0.82 us
  transfers between devices with their start and end apart: 14 -> 12, of which waited for: 5 -> 5; matrix products, arithmetic and copies ran while one was open for 0% -> 0% of each run, Pallas kernels for 5% -> 16%
where the time goes in v1:
time: 85.1 us; the launch traced here: 84.9 us
  waiting for transfers between devices  38.3 us (45%)
  starting transfers between devices  26.2 us (31%)
  Pallas kernels  18.9 us (22%)
    ppermute x6, waiting for transfers between devices, space_swap(): return lax.ppermute(value, 'space', [(i, i ^ flip) for i in range(count)])  26.2 us
    ppermute x6, starting transfers between devices, chain_swap(): return lax.ppermute(value, 'tm', pairs)  15.8 us
    ppermute x6, waiting for transfers between devices, chain_swap(): return lax.ppermute(value, 'tm', pairs)  12.1 us
    ppermute x6, starting transfers between devices, space_swap(): return lax.ppermute(value, 'space', [(i, i ^ flip) for i in range(count)])  10.4 us
    pallas_call x1, Pallas kernels, chain_grads(): pl.pallas_call(chain_grads_kernel, grid_spec=pltpu.PrefetchScalarGridSpec...  6.75 us
    pallas_call x1, Pallas kernels, chain_sums(): pl.pallas_call(chain_sums_kernel, grid_spec=pltpu.PrefetchScalarGridSpec(...  3.34 us
    pallas_call x1, Pallas kernels, space_grads(): pl.pallas_call(space_kernel, grid=(columns // SPACE_LANES,), in_specs=[ow...  3.24 us
    pallas_call x1, Pallas kernels, finish(): pl.pallas_call(functools.partial(finish_kernel, steps), grid_spec=pltpu.P...  3.07 us
  transfers between devices with their start and end apart: 12, of which 5 were waited for; matrix products, arithmetic and copies ran while one was open for 0% of the time, Pallas kernels for 16%

profile of v1, /device:TPU:1, one launch (start us, length us, event | category | flops | bytes accessed | tf_op | source)
XLA Modules:
  0.0 84.9 jit_solution(5921648983059813478)
XLA Ops:
  0.6 0.0 copy-start.3
  0.6 0.0 copy-start.2
  0.7 0.8 copy-done.5
  1.5 2.5 %pack.1 = (bf16[4,4,32,768]{3,2,1,0:T(8,128)(2,1)S(1)}, bf16[4,4,32,768]{3,2,1,0:T(8,128)(2,1)S(1)}, bf16[4,2,32,768]{3,2,1,0:T(8,128)(2,1)S(1)}, bf16[4,2,32,76...) custom-call(s32[128]{0:T(128)S(1)} %copy-done.5, bf16[8,32,1536]{2,1,0:T(8,128)(2,1)} %query_ref.7, ...), custom_call_target="tpu_custom_call" | custom-call | tf_op jit(solution)/shard_map/pack/pallas_call | solution.py:87
  4.0 2.6 %collective-permute-start.6 = (bf16[4,4,32,768]{3,2,1,0:T(8,128)(2,1)S(1)}, bf16[4,4,32,768]{3,2,1,0:T(8,128)(2,1)S(1)}, u32[]{:S(2)}, u32[]{:S(2)}) collective-permute-start(bf16[4,4,32,768]{3,2,1,0:T(8,128)(2,1)S(1)} %get-tuple-element.24), channel_id=1, source_target_pairs={{0,4},{4,0},{8,12},{12,8},{16,20},{20,16},{24,28},{28,24},{32,36},... | collective-permute-start | bytes 2359304 | tf_op jit(solution)/shard_map/ppermute | solution.py:34
  6.6 0.7 collective-permute-start.7
  7.3 1.0 %collective-permute-start = (bf16[4,2,32,768]{3,2,1,0:T(8,128)(2,1)S(1)}, bf16[4,2,32,768]{3,2,1,0:T(8,128)(2,1)S(1)}, u32[]{:S(2)}, u32[]{:S(2)}) collective-permute-start(bf16[4,2,32,768]{3,2,1,0:T(8,128)(2,1)S(1)} %get-tuple-element.17), channel_id=1, source_target_pairs={{0,1},{1,0},{2,3},{3,2},{4,5},{5,4},{6,7},{7,6},{8,9},{9,8},{10,11... | collective-permute-start | bytes 1179656 | tf_op jit(solution)/shard_map/ppermute | solution.py:39
  8.3 2.8 %collective-permute-start.1 = (bf16[4,2,32,768]{3,2,1,0:T(8,128)(2,1)S(1)}, bf16[4,2,32,768]{3,2,1,0:T(8,128)(2,1)S(1)}, u32[]{:S(2)}, u32[]{:S(2)}) collective-permute-start(bf16[4,2,32,768]{3,2,1,0:T(8,128)(2,1)S(1)} %get-tuple-element.18), channel_id=1, source_target_pairs={{0,2},{1,3},{2,0},{3,1},{4,6},{5,7},{6,4},{7,5},{8,10},{9,11},{10,... | collective-permute-start | bytes 1179656 | tf_op jit(solution)/shard_map/ppermute | solution.py:39
  11.1 0.5 collective-permute-start.2
  11.6 11.2 %collective-permute-done.6.got0_ref = bf16[4,4,32,768]{3,2,1,0:T(8,128)(2,1)S(1)} collective-permute-done((bf16[4,4,32,768]{3,2,1,0:T(8,128)(2,1)S(1)}, bf16[4,4,32,768]{3,2,1,0:T(8,128)(2,1)S(1)}, u32[]{:S(2)}, u32[]{:S(2)}) %collective-permute-start.6) | collective-permute-done | bytes 786464 | tf_op jit(solution)/shard_map/ppermute | solution.py:34
  22.8 0.0 collective-permute-done.7.got1_ref
  22.8 3.3 %chain_sums.1 = (f32[3,2,4,256]{3,2,1,0:T(4,128)S(1)}, f32[3,2,4,256]{3,2,1,0:T(4,128)S(1)}) custom-call(s32[128]{0:T(128)S(1)} %copy-done.5, s32[128]{0:T(128)S(1)} %copy-done.6, bf16[8,32,1536]{2,1,0:T(8,128)(2,1)S(1)} %copy-done, bf16[8,32,1536]{2,1,0:T(8,128)(2,1)S(1)} %copy-done.1, bf16[8,32,1536]{2,1,0:T(8,128)(2,1)S(1)} %copy-done.2, ...), custom_call_target="tpu_custom_call" | custom-call | tf_op jit(solution)/shard_map/chain_sums/pallas_call | solution.py:263
  26.2 6.0 %collective-permute-start.8 = (f32[3,2,4,256]{3,2,1,0:T(4,128)S(1)}, f32[3,2,4,256]{3,2,1,0:T(4,128)S(1)}, u32[]{:S(2)}, u32[]{:S(2)}) collective-permute-start(f32[3,2,4,256]{3,2,1,0:T(4,128)S(1)} %get-tuple-element.26.sums0_ref), channel_id=1, source_target_pairs={{0,4},{4,0},{8,12},{12,8},{16,20},{20,16},{24,28},{28,24},{32,36},... | collective-permute-start | bytes 73736 | tf_op jit(solution)/shard_map/ppermute | solution.py:34
  32.1 0.7 collective-permute-start.9
  32.8 0.9 %collective-permute-done.8.from0_ref = f32[3,2,4,256]{3,2,1,0:T(4,128)S(1)} collective-permute-done((f32[3,2,4,256]{3,2,1,0:T(4,128)S(1)}, f32[3,2,4,256]{3,2,1,0:T(4,128)S(1)}, u32[]{:S(2)}, u32[]{:S(2)}) %collective-permute-start.8) | collective-permute-done | bytes 24608 | tf_op jit(solution)/shard_map/ppermute | solution.py:34
  33.6 0.0 collective-permute-done.9.from1_ref
  33.6 6.8 %chain_grads.1 = (f32[3,8,32,768]{3,2,1,0:T(8,128)}, bf16[3,4,32,768]{3,2,1,0:T(8,128)(2,1)S(1)}, bf16[3,4,32,768]{3,2,1,0:T(8,128)(2,1)S(1)}) custom-call(s32[128]{0:T(128)S(1)} %copy-done.5, s32[128]{0:T(128)S(1)} %copy-done.6, bf16[8,32,1536]{2,1,0:T(8,128)(2,1)S(1)} %copy-done, bf16[8,32,1536]{2,1,0:T(8,128)(2,1)S(1)} %copy-done.1, ...), custom_call_target="tpu_custom_call" | custom-call | tf_op jit(solution)/shard_map/chain_grads/pallas_call | solution.py:279
  40.4 5.2 %collective-permute-start.10 = (bf16[3,4,32,768]{3,2,1,0:T(8,128)(2,1)S(1)}, bf16[3,4,32,768]{3,2,1,0:T(8,128)(2,1)S(1)}, u32[]{:S(2)}, u32[]{:S(2)}) collective-permute-start(bf16[3,4,32,768]{3,2,1,0:T(8,128)(2,1)S(1)} %get-tuple-element.29), channel_id=1, source_target_pairs={{0,4},{4,0},{8,12},{12,8},{16,20},{20,16},{24,28},{28,24},{32,36},... | collective-permute-start | bytes 1769480 | tf_op jit(solution)/shard_map/ppermute | solution.py:34
  45.6 0.7 collective-permute-start.11
  46.3 0.0 collective-permute-done.in1_ref
  46.3 0.0 collective-permute-done.1.in2_ref
  46.3 0.2 collective-permute-done.2.in3_ref
  46.5 3.2 %space_grads.1 = (bf16[3,2,32,768]{3,2,1,0:T(8,128)(2,1)S(1)}, bf16[3,2,32,768]{3,2,1,0:T(8,128)(2,1)S(1)}, bf16[3,2,32,768]{3,2,1,0:T(8,128)(2,1)S(1)}, bf16[3,2,32,768]{3,2,1,0:T(8,128)(2,1)S(1)}) custom-call(bf16[8,32,1536]{2,1,0:T(8,128)(2,1)S(1)} %copy-done, bf16[8,32,1536]{2,1,0:T(8,128)(2,1)S(1)} %copy-done.1, bf16[8,32,1536]{2,1,0:T(8,128)(2,1)S(1)} %copy-done.2, ...), custom_call_target="tpu_custom_call" | custom-call | flops 400000000 | bytes 4000000 | tf_op jit(solution)/shard_map/space_grads/pallas_call | solution.py:323
  49.8 2.9 %collective-permute-start.3 = (bf16[3,2,32,768]{3,2,1,0:T(8,128)(2,1)S(1)}, bf16[3,2,32,768]{3,2,1,0:T(8,128)(2,1)S(1)}, u32[]{:S(2)}, u32[]{:S(2)}) collective-permute-start(bf16[3,2,32,768]{3,2,1,0:T(8,128)(2,1)S(1)} %get-tuple-element.21), channel_id=1, source_target_pairs={{0,1},{1,0},{2,3},{3,2},{4,5},{5,4},{6,7},{7,6},{8,9},{9,8},{10,11... | collective-permute-start | bytes 884744 | tf_op jit(solution)/shard_map/ppermute | solution.py:39
  52.6 2.8 %collective-permute-start.4 = (bf16[3,2,32,768]{3,2,1,0:T(8,128)(2,1)S(1)}, bf16[3,2,32,768]{3,2,1,0:T(8,128)(2,1)S(1)}, u32[]{:S(2)}, u32[]{:S(2)}) collective-permute-start(bf16[3,2,32,768]{3,2,1,0:T(8,128)(2,1)S(1)} %get-tuple-element.22), channel_id=1, source_target_pairs={{0,2},{1,3},{2,0},{3,1},{4,6},{5,7},{6,4},{7,5},{8,10},{9,11},{10,... | collective-permute-start | bytes 884744 | tf_op jit(solution)/shard_map/ppermute | solution.py:39
  55.4 0.5 collective-permute-start.5
  55.9 0.0 collective-permute-done.3.refs_1_
  55.9 19.7 %collective-permute-done.4.refs_2_ = bf16[3,2,32,768]{3,2,1,0:T(8,128)(2,1)S(1)} collective-permute-done((bf16[3,2,32,768]{3,2,1,0:T(8,128)(2,1)S(1)}, bf16[3,2,32,768]{3,2,1,0:T(8,128)(2,1)S(1)}, u32[]{:S(2)}, u32[]{:S(2)}) %collective-permute-start.4) | collective-permute-done | bytes 294944 | tf_op jit(solution)/shard_map/ppermute | solution.py:39
  75.5 6.3 %collective-permute-done.5.refs_3_ = bf16[3,2,32,768]{3,2,1,0:T(8,128)(2,1)S(1)} collective-permute-done((bf16[3,2,32,768]{3,2,1,0:T(8,128)(2,1)S(1)}, bf16[3,2,32,768]{3,2,1,0:T(8,128)(2,1)S(1)}, u32[]{:S(2)}, u32[]{:S(2)}) %collective-permute-start.5) | collective-permute-done | bytes 294944 | tf_op jit(solution)/shard_map/ppermute | solution.py:39
  81.9 0.0 collective-permute-done.10.refs_5_
  81.9 0.0 collective-permute-done.11.refs_6_
  81.9 3.1 %finish.1 = (bf16[8,32,1536]{2,1,0:T(8,128)(2,1)}, bf16[8,32,1536]{2,1,0:T(8,128)(2,1)}, bf16[8,32,1536]{2,1,0:T(8,128)(2,1)}) custom-call(s32[128]{0:T(128)S(1)} %copy-done.5, bf16[3,2,32,768]{3,2,1,0:T(8,128)(2,1)S(1)} %get-tuple-element.20.refs_0_, bf16[3,2,32,768]{3,2,1,0:T(8,128)(2,1)S(1)} %collective-permute-done.3.refs_1_, ...), custom_call_target="tpu_custom_call" | custom-call | tf_op jit(solution)/shard_map/finish/pallas_call | solution.py:373
  (11 shorter events, 0.0 us)
Async XLA Ops:
  0.6 22.2 %copy-start.3 = (bf16[8,32,1536]{2,1,0:T(8,128)(2,1)S(1)}, bf16[8,32,1536]{2,1,0:T(8,128)(2,1)}, u32[]{:S(2)}) copy-start(bf16[8,32,1536]{2,1,0:T(8,128)(2,1)} %grad_ref.7) | copy-start | bytes 2359300
  0.6 22.2 %copy-start.2 = (bf16[8,32,1536]{2,1,0:T(8,128)(2,1)S(1)}, bf16[8,32,1536]{2,1,0:T(8,128)(2,1)}, u32[]{:S(2)}) copy-start(bf16[8,32,1536]{2,1,0:T(8,128)(2,1)} %value_ref.7) | copy-start | bytes 2359300
  0.7 22.2 %copy-start.1 = (bf16[8,32,1536]{2,1,0:T(8,128)(2,1)S(1)}, bf16[8,32,1536]{2,1,0:T(8,128)(2,1)}, u32[]{:S(2)}) copy-start(bf16[8,32,1536]{2,1,0:T(8,128)(2,1)} %key_ref.7) | copy-start | bytes 2359300
  0.7 22.1 %copy-start = (bf16[8,32,1536]{2,1,0:T(8,128)(2,1)S(1)}, bf16[8,32,1536]{2,1,0:T(8,128)(2,1)}, u32[]{:S(2)}) copy-start(bf16[8,32,1536]{2,1,0:T(8,128)(2,1)} %query_ref.7) | copy-start | bytes 2359300
  0.7 0.8 copy-start.5
  1.5 21.3 %copy-start.6 = (s32[128]{0:T(128)S(1)}, s32[128]{0:T(128)}, u32[]{:S(2)}) copy-start(s32[128]{0:T(128)} %lookback_ref.3) | copy-start | bytes 1540
  4.0 18.8 %collective-permute-start.6 = (bf16[4,4,32,768]{3,2,1,0:T(8,128)(2,1)S(1)}, bf16[4,4,32,768]{3,2,1,0:T(8,128)(2,1)S(1)}, u32[]{:S(2)}, u32[]{:S(2)}) collective-permute-start(bf16[4,4,32,768]{3,2,1,0:T(8,128)(2,1)S(1)} %get-tuple-element.24), channel_id=1, source_target_pairs={{0,4},{4,0},{8,12},{12,8},{16,20},{20,16},{24,28},{28,24},{32,36},... | collective-permute-start | bytes 2359304 | tf_op jit(solution)/shard_map/ppermute | solution.py:34
  6.6 16.2 %collective-permute-start.7 = (bf16[4,4,32,768]{3,2,1,0:T(8,128)(2,1)S(1)}, bf16[4,4,32,768]{3,2,1,0:T(8,128)(2,1)S(1)}, u32[]{:S(2)}, u32[]{:S(2)}) collective-permute-start(bf16[4,4,32,768]{3,2,1,0:T(8,128)(2,1)S(1)} %get-tuple-element.25), channel_id=1, source_target_pairs={{4,8},{8,4},{12,16},{16,12},{20,24},{24,20},{28,32},{32,28},{36,40... | collective-permute-start | bytes 2359304 | tf_op jit(solution)/shard_map/ppermute | solution.py:34
  7.3 39.0 %collective-permute-start = (bf16[4,2,32,768]{3,2,1,0:T(8,128)(2,1)S(1)}, bf16[4,2,32,768]{3,2,1,0:T(8,128)(2,1)S(1)}, u32[]{:S(2)}, u32[]{:S(2)}) collective-permute-start(bf16[4,2,32,768]{3,2,1,0:T(8,128)(2,1)S(1)} %get-tuple-element.17), channel_id=1, source_target_pairs={{0,1},{1,0},{2,3},{3,2},{4,5},{5,4},{6,7},{7,6},{8,9},{9,8},{10,11... | collective-permute-start | bytes 1179656 | tf_op jit(solution)/shard_map/ppermute | solution.py:39
  8.3 38.0 %collective-permute-start.1 = (bf16[4,2,32,768]{3,2,1,0:T(8,128)(2,1)S(1)}, bf16[4,2,32,768]{3,2,1,0:T(8,128)(2,1)S(1)}, u32[]{:S(2)}, u32[]{:S(2)}) collective-permute-start(bf16[4,2,32,768]{3,2,1,0:T(8,128)(2,1)S(1)} %get-tuple-element.18), channel_id=1, source_target_pairs={{0,2},{1,3},{2,0},{3,1},{4,6},{5,7},{6,4},{7,5},{8,10},{9,11},{10,... | collective-permute-start | bytes 1179656 | tf_op jit(solution)/shard_map/ppermute | solution.py:39
  11.1 35.4 %collective-permute-start.2 = (bf16[4,2,32,768]{3,2,1,0:T(8,128)(2,1)S(1)}, bf16[4,2,32,768]{3,2,1,0:T(8,128)(2,1)S(1)}, u32[]{:S(2)}, u32[]{:S(2)}) collective-permute-start(bf16[4,2,32,768]{3,2,1,0:T(8,128)(2,1)S(1)} %get-tuple-element.19), channel_id=1, source_target_pairs={{0,3},{1,2},{2,1},{3,0},{4,7},{5,6},{6,5},{7,4},{8,11},{9,10},{10,... | collective-permute-start | bytes 1179656 | tf_op jit(solution)/shard_map/ppermute | solution.py:39
  26.2 7.5 %collective-permute-start.8 = (f32[3,2,4,256]{3,2,1,0:T(4,128)S(1)}, f32[3,2,4,256]{3,2,1,0:T(4,128)S(1)}, u32[]{:S(2)}, u32[]{:S(2)}) collective-permute-start(f32[3,2,4,256]{3,2,1,0:T(4,128)S(1)} %get-tuple-element.26.sums0_ref), channel_id=1, source_target_pairs={{0,4},{4,0},{8,12},{12,8},{16,20},{20,16},{24,28},{28,24},{32,36},... | collective-permute-start | bytes 73736 | tf_op jit(solution)/shard_map/ppermute | solution.py:34
  32.1 1.5 %collective-permute-start.9 = (f32[3,2,4,256]{3,2,1,0:T(4,128)S(1)}, f32[3,2,4,256]{3,2,1,0:T(4,128)S(1)}, u32[]{:S(2)}, u32[]{:S(2)}) collective-permute-start(f32[3,2,4,256]{3,2,1,0:T(4,128)S(1)} %get-tuple-element.27.sums1_ref), channel_id=1, source_target_pairs={{4,8},{8,4},{12,16},{16,12},{20,24},{24,20},{28,32},{32,28},{36,40... | collective-permute-start | bytes 73736 | tf_op jit(solution)/shard_map/ppermute | solution.py:34
  40.4 41.5 %copy-start.4 = (f32[3,8,32,768]{3,2,1,0:T(8,128)S(1)}, f32[3,8,32,768]{3,2,1,0:T(8,128)}, u32[]{:S(2)}) copy-start(f32[3,8,32,768]{3,2,1,0:T(8,128)} %get-tuple-element.28.refs_4_) | copy-start | bytes 7077892
  40.4 41.5 %collective-permute-start.10 = (bf16[3,4,32,768]{3,2,1,0:T(8,128)(2,1)S(1)}, bf16[3,4,32,768]{3,2,1,0:T(8,128)(2,1)S(1)}, u32[]{:S(2)}, u32[]{:S(2)}) collective-permute-start(bf16[3,4,32,768]{3,2,1,0:T(8,128)(2,1)S(1)} %get-tuple-element.29), channel_id=1, source_target_pairs={{0,4},{4,0},{8,12},{12,8},{16,20},{20,16},{24,28},{28,24},{32,36},... | collective-permute-start | bytes 1769480 | tf_op jit(solution)/shard_map/ppermute | solution.py:34
  45.6 36.3 %collective-permute-start.11 = (bf16[3,4,32,768]{3,2,1,0:T(8,128)(2,1)S(1)}, bf16[3,4,32,768]{3,2,1,0:T(8,128)(2,1)S(1)}, u32[]{:S(2)}, u32[]{:S(2)}) collective-permute-start(bf16[3,4,32,768]{3,2,1,0:T(8,128)(2,1)S(1)} %get-tuple-element.30), channel_id=1, source_target_pairs={{4,8},{8,4},{12,16},{16,12},{20,24},{24,20},{28,32},{32,28},{36,40... | collective-permute-start | bytes 1769480 | tf_op jit(solution)/shard_map/ppermute | solution.py:34
  49.8 6.1 %collective-permute-start.3 = (bf16[3,2,32,768]{3,2,1,0:T(8,128)(2,1)S(1)}, bf16[3,2,32,768]{3,2,1,0:T(8,128)(2,1)S(1)}, u32[]{:S(2)}, u32[]{:S(2)}) collective-permute-start(bf16[3,2,32,768]{3,2,1,0:T(8,128)(2,1)S(1)} %get-tuple-element.21), channel_id=1, source_target_pairs={{0,1},{1,0},{2,3},{3,2},{4,5},{5,4},{6,7},{7,6},{8,9},{9,8},{10,11... | collective-permute-start | bytes 884744 | tf_op jit(solution)/shard_map/ppermute | solution.py:39
  52.6 22.9 %collective-permute-start.4 = (bf16[3,2,32,768]{3,2,1,0:T(8,128)(2,1)S(1)}, bf16[3,2,32,768]{3,2,1,0:T(8,128)(2,1)S(1)}, u32[]{:S(2)}, u32[]{:S(2)}) collective-permute-start(bf16[3,2,32,768]{3,2,1,0:T(8,128)(2,1)S(1)} %get-tuple-element.22), channel_id=1, source_target_pairs={{0,2},{1,3},{2,0},{3,1},{4,6},{5,7},{6,4},{7,5},{8,10},{9,11},{10,... | collective-permute-start | bytes 884744 | tf_op jit(solution)/shard_map/ppermute | solution.py:39
  55.4 26.4 %collective-permute-start.5 = (bf16[3,2,32,768]{3,2,1,0:T(8,128)(2,1)S(1)}, bf16[3,2,32,768]{3,2,1,0:T(8,128)(2,1)S(1)}, u32[]{:S(2)}, u32[]{:S(2)}) collective-permute-start(bf16[3,2,32,768]{3,2,1,0:T(8,128)(2,1)S(1)} %get-tuple-element.23), channel_id=1, source_target_pairs={{0,3},{1,2},{2,1},{3,0},{4,7},{5,6},{6,5},{7,4},{8,11},{9,10},{10,... | collective-permute-start | bytes 884744 | tf_op jit(solution)/shard_map/ppermute | solution.py:39

commit v2 on v1

--- a/solution.py
+++ b/solution.py
@@ -2,6 +2,7 @@
 
 import jax
 import jax.numpy as jnp
+import numpy as np
 from jax import lax
 from jax.experimental import pallas as pl
 from jax.experimental.pallas import tpu as pltpu
@@ -92,7 +93,7 @@
         scratch_shapes=[pltpu.SemaphoreType.DMA((20,))],
         compiler_params=params(),
         name="pack",
-    )(group_order, *[pltpu.with_memory_space_constraint(x, pltpu.HBM) for x in (query, key, value, grad)])
+    )(*[pltpu.with_memory_space_constraint(x, pltpu.HBM) for x in (group_order, query, key, value, grad)])
     return outs[:2], outs[2:]
 
 
@@ -150,7 +151,9 @@
 class Side:
     def __init__(self, side, order_ref, lookback_ref, locals_, before_ref, after_ref):
         self.locals, self.before, self.after = locals_, before_ref, after_ref
-        frames, self.patches, self.lanes = locals_[0].shape
+        frames, self.patches, width = locals_[0].shape
+        self.lanes = CHAIN_LANES
+        self.first = width // 2
         self.half = frames // 2
         self.rows = self.half * BAND
         self.heads = self.lanes // HD
@@ -171,11 +174,12 @@
     def flat(self, piece):
         return piece.reshape(self.rows, self.lanes)
 
-    def load(self, band):
+    def load(self, quad, band):
         at = pl.ds(band * BAND, BAND)
-        query, key, value, grad = (self.flat(ref[self.mine, at]) for ref in self.locals)
-        key_before, value_before = (self.flat(self.before[index, :, at]) for index in (0, 1))
-        query_after, grad_after = (self.flat(self.after[index, :, at]) for index in (2, 3))
+        near, far = pl.ds(self.first + quad * self.lanes, self.lanes), pl.ds(quad * self.lanes, self.lanes)
+        query, key, value, grad = (self.flat(ref[self.mine, at, near]) for ref in self.locals)
+        key_before, value_before = (self.flat(self.before[index, :, at, far]) for index in (0, 1))
+        query_after, grad_after = (self.flat(self.after[index, :, at, far]) for index in (2, 3))
         keys = jnp.concatenate([key, key_before], axis=0)
         values = jnp.concatenate([value, value_before], axis=0)
         near = (keys, scale(query), per_head(grad))
@@ -197,10 +201,10 @@
 ):
     sides = both_sides(order_ref, lookback_ref, (query_ref, key_ref, value_ref, grad_ref), got0_ref, got1_ref)
     for side, near_out, skip_out in zip(sides, (out0_ref, out1_ref), (out1_ref, out0_ref)):
-        for band in range(side.patches // BAND):
-            near, skip = side.load(band)
-            near_out[0, band, 0:1], near_out[0, band, 1:2] = sums(*near[3:])
-            skip_out[0, band, 2:3], skip_out[0, band, 3:4] = sums(*skip[3:])
+        for quad, band in np.ndindex(*out0_ref.shape[:2]):
+            near, skip = side.load(quad, band)
+            near_out[quad, band, 0:1], near_out[quad, band, 1:2] = sums(*near[3:])
+            skip_out[quad, band, 2:3], skip_out[quad, band, 3:4] = sums(*skip[3:])
 
 
 def chain_grads_kernel(
@@ -224,71 +228,55 @@
     mine, others, outs = (sums0_ref, sums1_ref), (from0_ref, from1_ref), (out0_ref, out1_ref)
     for number, side in enumerate(sides):
         rows, tall = side.rows, (side.half, BAND, side.lanes)
-        for band in range(side.patches // BAND):
-            at = pl.ds(band * BAND, BAND)
-            near, skip = side.load(band)
+        for quad, band in np.ndindex(*sums0_ref.shape[:2]):
+            at, far = pl.ds(band * BAND, BAND), pl.ds(quad * CHAIN_LANES, CHAIN_LANES)
+            near, skip = side.load(quad, band)
 
             def whole_sums(row):
                 place = number if row == 0 else 1 - number
                 ours, theirs = mine[place], others[place]
                 return [
-                    ours[0, band, row + k : row + k + 1] + theirs[0, band, 2 - row + k : 3 - row + k] for k in (0, 1)
+                    ours[quad, band, row + k : row + k + 1] + theirs[quad, band, 2 - row + k : 3 - row + k] for k in (0, 1)
                 ]
 
             dq, dk, dv = gradients(*near, *whole_sums(0))
             dq_after, dk_before, dv_before = gradients(*skip, *whole_sums(2))
-            own_ref[0, side.mine, at] = dq.reshape(tall)
-            own_ref[1, side.mine, at] = dk[:rows].reshape(tall)
-            own_ref[2, side.mine, at] = dv[:rows].reshape(tall)
+            own_ref[0, side.mine, at, far] = dq.reshape(tall)
+            own_ref[1, side.mine, at, far] = dk[:rows].reshape(tall)
+            own_ref[2, side.mine, at, far] = dv[:rows].reshape(tall)
             back, on = outs[number], outs[1 - number]
-            back[0, :, at] = (dk[rows:] + dk_before).astype(BF16).reshape(tall)
-            back[1, :, at] = (dv[rows:] + dv_before).astype(BF16).reshape(tall)
-            on[2, :, at] = dq_after.astype(BF16).reshape(tall)
-
-
-def chain_specs(query):
+            back[0, :, at, far] = (dk[rows:] + dk_before).astype(BF16).reshape(tall)
+            back[1, :, at, far] = (dv[rows:] + dv_before).astype(BF16).reshape(tall)
+            on[2, :, at, far] = dq_after.astype(BF16).reshape(tall)
+
+
+def chain_call(kernel, out_shape, name, *operands):
+    return pl.pallas_call(
+        kernel,
+        in_specs=[pl.BlockSpec(memory_space=pltpu.SMEM)] * 2
+        + [pl.BlockSpec(memory_space=pltpu.VMEM)] * (len(operands) - 2),
+        out_specs=[pl.BlockSpec(memory_space=pltpu.VMEM)] * len(out_shape),
+        out_shape=out_shape,
+        compiler_params=params(),
+        name=name,
+    )(*operands)
+
+
+def chain_sums(group_order, lookback, query, key, value, grad, got0, got1):
     frames, patches, width = query.shape
-    half, columns = frames // 2, width // 2
-    steps = columns // CHAIN_LANES
-    bands = patches // BAND
-    wide = CHAIN_LANES // HD * half * BAND
-    whole = pl.BlockSpec((frames, patches, CHAIN_LANES), lambda i, *_: (0, 0, steps + i))
-    got = pl.BlockSpec((4, half, patches, CHAIN_LANES), lambda i, *_: (0, 0, 0, i))
-    part = pl.BlockSpec((1, bands, 4, wide), lambda i, *_: (i, 0, 0, 0))
-    return steps, [whole] * 4 + [got] * 2, part, jax.ShapeDtypeStruct((steps, bands, 4, wide), F32)
-
-
-def chain_sums(group_order, lookback, query, key, value, grad, got0, got1):
-    steps, in_specs, part, shape = chain_specs(query)
-    return pl.pallas_call(
-        chain_sums_kernel,
-        grid_spec=pltpu.PrefetchScalarGridSpec(
-            num_scalar_prefetch=2, grid=(steps,), in_specs=in_specs, out_specs=[part] * 2
-        ),
-        out_shape=[shape] * 2,
-        compiler_params=params(),
-        name="chain_sums",
-    )(group_order, lookback, query, key, value, grad, got0, got1)
+    steps, bands = width // 2 // CHAIN_LANES, patches // BAND
+    shape = jax.ShapeDtypeStruct((steps, bands, 4, CHAIN_LANES // HD * frames // 2 * BAND), F32)
+    operands = (group_order, lookback, query, key, value, grad, got0, got1)
+    return chain_call(chain_sums_kernel, [shape] * 2, "chain_sums", *operands)
 
 
 def chain_grads(group_order, lookback, query, key, value, grad, got0, got1, ours, theirs):
     frames, patches, width = query.shape
     half, columns = frames // 2, width // 2
-    steps, in_specs, part, _ = chain_specs(query)
     sent = jax.ShapeDtypeStruct((3, half, patches, columns), BF16)
-    return pl.pallas_call(
-        chain_grads_kernel,
-        grid_spec=pltpu.PrefetchScalarGridSpec(
-            num_scalar_prefetch=2,
-            grid=(steps,),
-            in_specs=in_specs + [part] * 4,
-            out_specs=[pl.BlockSpec((3, frames, patches, CHAIN_LANES), lambda i, *_: (0, 0, 0, i))]
-            + [pl.BlockSpec((3, half, patches, CHAIN_LANES), lambda i, *_: (0, 0, 0, i))] * 2,
-        ),
-        out_shape=[jax.ShapeDtypeStruct((3, frames, patches, columns), F32), sent, sent],
-        compiler_params=params(),
-        name="chain_grads",
-    )(group_order, lookback, query, key, value, grad, got0, got1, *ours, *theirs)
+    shapes = [jax.ShapeDtypeStruct((3, frames, patches, columns), F32), sent, sent]
+    operands = (group_order, lookback, query, key, value, grad, got0, got1, *ours, *theirs)
+    return chain_call(chain_grads_kernel, shapes, "chain_grads", *operands)
 
 
 def space_kernel(
@@ -334,70 +322,72 @@
     )(query, key, value, grad, *arrived)
 
 
-def finish_kernel(steps, order_ref, *refs):
-    parts, (own_ref, got0_ref, got1_ref), outs = refs[:4], refs[4:7], refs[7:]
-    step = pl.program_id(0)
-    share, frames = parts[0].shape[1], own_ref.shape[1]
-    half = frames // 2
-
-    @pl.when(step < steps)
-    def _():
-        me = lax.axis_index("space")
-        for flip, part_ref in enumerate(parts):
-            place = pl.ds(share * (me ^ flip), share)
-            for index, out_ref in enumerate(outs):
-                out_ref[place] = part_ref[index]
-
-    @pl.when(step >= steps)
-    def _():
-        slots = side_slots(order_ref)
-        for slot, query_ref, key_ref in zip(slots, (got0_ref, got1_ref), (got1_ref, got0_ref)):
-            mine = pl.ds(slot * half, half)
-            arrived = (query_ref[2], key_ref[0], key_ref[1])
-            for index, (out_ref, piece) in enumerate(zip(outs, arrived)):
-                out_ref[mine] = (own_ref[index, mine] + piece.astype(F32)).astype(BF16)
-
-
-def finish(group_order, parts, own, got0, got1):
+def finish_chain_kernel(order_ref, own_ref, got0_ref, got1_ref, *outs):
+    half = own_ref.shape[1] // 2
+    slots = side_slots(order_ref)
+    for slot, query_ref, key_ref in zip(slots, (got0_ref, got1_ref), (got1_ref, got0_ref)):
+        mine = pl.ds(slot * half, half)
+        arrived = (query_ref[2], key_ref[0], key_ref[1])
+        for index, (out_ref, piece) in enumerate(zip(outs, arrived)):
+            out_ref[mine] = (own_ref[index, mine] + piece.astype(F32)).astype(BF16)
+
+
+def finish_chain(group_order, own, got0, got1):
     _, frames, patches, columns = own.shape
     wide = 3 * LANES
     steps = columns // wide
-    share = parts[0].shape[1]
-
-    def early(i, *_):
-        return (0, 0, 0, jnp.minimum(i, steps - 1))
-
-    def late(i, *_):
-        return (0, 0, 0, jnp.maximum(i - steps, 0))
-
     return pl.pallas_call(
-        functools.partial(finish_kernel, steps),
+        finish_chain_kernel,
         grid_spec=pltpu.PrefetchScalarGridSpec(
             num_scalar_prefetch=1,
-            grid=(2 * steps,),
-            in_specs=[pl.BlockSpec((3, share, patches, wide), early)] * 4
-            + [pl.BlockSpec((3, frames, patches, wide), late)]
-            + [pl.BlockSpec((3, frames // 2, patches, wide), late)] * 2,
-            out_specs=[pl.BlockSpec((frames, patches, wide), lambda i, *_: (0, 0, i))] * 3,
+            grid=(steps,),
+            in_specs=[pl.BlockSpec((3, frames, patches, wide), lambda i, *_: (0, 0, 0, i))]
+            + [pl.BlockSpec((3, frames // 2, patches, wide), lambda i, *_: (0, 0, 0, i))] * 2,
+            out_specs=[pl.BlockSpec((frames, patches, wide), lambda i, *_: (0, 0, steps + i))] * 3,
         ),
         out_shape=[jax.ShapeDtypeStruct((frames, patches, 2 * columns), BF16)] * 3,
         compiler_params=params(),
-        name="finish",
-    )(group_order, *parts, own, got0, got1)
+        name="finish_chain",
+    )(group_order, own, got0, got1)
+
+
+def finish_space_kernel(*refs):
+    parts, outs = refs[:4], refs[7:]
+    me = lax.axis_index("space")
+    share = parts[0].shape[1]
+    for flip, part_ref in enumerate(parts):
+        place = pl.ds(share * (me ^ flip), share)
+        for index, out_ref in enumerate(outs):
+            out_ref[place] = part_ref[index]
+
+
+def finish_space(parts, outs):
+    _, share, patches, columns = parts[0].shape
+    frames, wide = 4 * share, 3 * LANES
+    return pl.pallas_call(
+        finish_space_kernel,
+        grid=(columns // wide,),
+        in_specs=[pl.BlockSpec((3, share, patches, wide), lambda i: (0, 0, 0, i))] * 4
+        + [pl.BlockSpec(memory_space=pl.ANY)] * 3,
+        out_specs=[pl.BlockSpec((frames, patches, wide), lambda i: (0, 0, i))] * 3,
+        out_shape=[jax.ShapeDtypeStruct(array.shape, BF16) for array in outs],
+        input_output_aliases={4: 0, 5: 1, 6: 2},
+        compiler_params=params(),
+        name="finish_space",
+    )(*parts, *outs)
 
 
 def on_device(query, key, value, grad_out, group_order, lookback):
     chain, sent = pack(group_order, query, key, value, grad_out)
-    sent = list(sent)
+    arrived = [space_swap(part, flip) for flip, part in enumerate(sent, 1)]
     got = [chain_swap(part, phase) for phase, part in enumerate(chain)]
-    arrived = [space_swap(part, flip) for flip, part in enumerate(sent, 1)]
     ours = chain_sums(group_order, lookback, query, key, value, grad_out, *got)
     theirs = [chain_swap(part, phase) for phase, part in enumerate(ours)]
     own, *back = chain_grads(group_order, lookback, query, key, value, grad_out, *got, ours, theirs)
-    back = [chain_swap(part, phase) for phase, part in enumerate(back)]
     results = space_grads(query, key, value, grad_out, arrived)
     parts = [results[0]] + [space_swap(part, flip) for flip, part in enumerate(results[1:], 1)]
-    return tuple(finish(group_order, parts, own, *back))
+    back = [chain_swap(part, phase) for phase, part in enumerate(back)]
+    return tuple(finish_space(parts, finish_chain(group_order, own, *back)))
 
 
 def solution(mesh):

time: 85.1 us -> 81.9 us (0.962)
  starting transfers between devices: 26.2 us -> 25.2 us
  waiting for transfers between devices: 38.3 us -> 37.3 us
    ppermute x6, waiting for transfers between devices: 26.2 us -> 24.5 us  [space_swap(): return lax.ppermute(value, 'space', [(i, i ^ flip) for i in range(count)])]
    ppermute x6, starting transfers between devices: 10.4 us -> 9.44 us  [space_swap(): return lax.ppermute(value, 'space', [(i, i ^ flip) for i in range(count)])]
    pallas_call x3 -> x4, Pallas kernels: 13.2 us -> 12.3 us  [the longest x2 9.13 us: chain_call(): pl.pallas_call(kernel, in_specs=[pl.BlockSpec(memory_space=pltpu.SMEM)] *...]
  transfers between devices with their start and end apart: 12 -> 12, of which waited for: 5 -> 6; matrix products, arithmetic and copies ran while one was open for 0% -> 0% of each run, Pallas kernels for 16% -> 18%
where the time goes in v2:
time: 81.9 us; the launch traced here: 81.7 us
  waiting for transfers between devices  37.3 us (46%)
  starting transfers between devices  25.2 us (31%)
  Pallas kernels  18.4 us (22%)
    ppermute x6, waiting for transfers between devices, space_swap(): return lax.ppermute(value, 'space', [(i, i ^ flip) for i in range(count)])  24.5 us
    ppermute x6, starting transfers between devices, chain_swap(): return lax.ppermute(value, 'tm', pairs)  15.7 us
    ppermute x6, waiting for transfers between devices, chain_swap(): return lax.ppermute(value, 'tm', pairs)  12.7 us
    ppermute x6, starting transfers between devices, space_swap(): return lax.ppermute(value, 'space', [(i, i ^ flip) for i in range(count)])  9.44 us
    pallas_call x2, Pallas kernels, chain_call(): pl.pallas_call(kernel, in_specs=[pl.BlockSpec(memory_space=pltpu.SMEM)] *...  9.13 us
    pallas_call x1, Pallas kernels, space_grads(): pl.pallas_call(space_kernel, grid=(columns // SPACE_LANES,), in_specs=[ow...  3.23 us
    pallas_call x1, Pallas kernels, pack(): pl.pallas_call(pack_kernel, out_shape=(chain, chain, space, space, space)...  2.89 us
    pallas_call x1, Pallas kernels, finish_chain(): pl.pallas_call(finish_chain_kernel, grid_spec=pltpu.PrefetchScalarGridSpe...  1.96 us
  transfers between devices with their start and end apart: 12, of which 6 were waited for; matrix products, arithmetic and copies ran while one was open for 0% of the time, Pallas kernels for 18%

profile of v2, /device:TPU:1, one launch (start us, length us, event | category | flops | bytes accessed | tf_op | source)
XLA Modules:
  0.0 81.7 jit_solution(13744996164881685907)
XLA Ops:
  0.6 0.0 copy-start.5
  0.6 0.0 copy-start.3
  0.7 2.9 %pack.1 = (bf16[4,4,32,768]{3,2,1,0:T(8,128)(2,1)S(1)}, bf16[4,4,32,768]{3,2,1,0:T(8,128)(2,1)S(1)}, bf16[4,2,32,768]{3,2,1,0:T(8,128)(2,1)S(1)}, bf16[4,2,32,76...) custom-call(s32[128]{0:T(128)} %order_ref.7, bf16[8,32,1536]{2,1,0:T(8,128)(2,1)} %query_ref.7, ...), custom_call_target="tpu_custom_call" | custom-call | tf_op jit(solution)/shard_map/pack/pallas_call | solution.py:88
  3.6 2.6 %collective-permute-start.6 = (bf16[4,4,32,768]{3,2,1,0:T(8,128)(2,1)S(1)}, bf16[4,4,32,768]{3,2,1,0:T(8,128)(2,1)S(1)}, u32[]{:S(2)}, u32[]{:S(2)}) collective-permute-start(bf16[4,4,32,768]{3,2,1,0:T(8,128)(2,1)S(1)} %get-tuple-element.27), channel_id=1, source_target_pairs={{0,4},{4,0},{8,12},{12,8},{16,20},{20,16},{24,28},{28,24},{32,36},... | collective-permute-start | bytes 2359304 | tf_op jit(solution)/shard_map/ppermute | solution.py:35
  6.1 0.7 collective-permute-start.7
  6.8 1.0 %collective-permute-start = (bf16[4,2,32,768]{3,2,1,0:T(8,128)(2,1)S(1)}, bf16[4,2,32,768]{3,2,1,0:T(8,128)(2,1)S(1)}, u32[]{:S(2)}, u32[]{:S(2)}) collective-permute-start(bf16[4,2,32,768]{3,2,1,0:T(8,128)(2,1)S(1)} %get-tuple-element.20), channel_id=1, source_target_pairs={{0,1},{1,0},{2,3},{3,2},{4,5},{5,4},{6,7},{7,6},{8,9},{9,8},{10,11... | collective-permute-start | bytes 1179656 | tf_op jit(solution)/shard_map/ppermute | solution.py:40
  7.9 2.8 %collective-permute-start.1 = (bf16[4,2,32,768]{3,2,1,0:T(8,128)(2,1)S(1)}, bf16[4,2,32,768]{3,2,1,0:T(8,128)(2,1)S(1)}, u32[]{:S(2)}, u32[]{:S(2)}) collective-permute-start(bf16[4,2,32,768]{3,2,1,0:T(8,128)(2,1)S(1)} %get-tuple-element.21), channel_id=1, source_target_pairs={{0,2},{1,3},{2,0},{3,1},{4,6},{5,7},{6,4},{7,5},{8,10},{9,11},{10,... | collective-permute-start | bytes 1179656 | tf_op jit(solution)/shard_map/ppermute | solution.py:40
  10.7 0.5 collective-permute-start.2
  11.1 11.2 %collective-permute-done.6.got0_ref = bf16[4,4,32,768]{3,2,1,0:T(8,128)(2,1)S(1)} collective-permute-done((bf16[4,4,32,768]{3,2,1,0:T(8,128)(2,1)S(1)}, bf16[4,4,32,768]{3,2,1,0:T(8,128)(2,1)S(1)}, u32[]{:S(2)}, u32[]{:S(2)}) %collective-permute-start.6) | collective-permute-done | bytes 786464 | tf_op jit(solution)/shard_map/ppermute | solution.py:35
  22.4 0.0 collective-permute-done.7.got1_ref
  22.4 2.7 %chain_sums.1 = (f32[3,2,4,256]{3,2,1,0:T(4,128)S(1)}, f32[3,2,4,256]{3,2,1,0:T(4,128)S(1)}) custom-call(s32[128]{0:T(128)S(1)} %copy-done.5, s32[128]{0:T(128)S(1)} %copy-done.6, bf16[8,32,1536]{2,1,0:T(8,128)(2,1)S(1)} %copy-done, bf16[8,32,1536]{2,1,0:T(8,128)(2,1)S(1)} %copy-done.1, bf16[8,32,1536]{2,1,0:T(8,128)(2,1)S(1)} %copy-done.2, ...), custom_call_target="tpu_custom_call" | custom-call | tf_op jit(solution)/shard_map/chain_sums/pallas_call | solution.py:254
  25.1 5.9 %collective-permute-start.8 = (f32[3,2,4,256]{3,2,1,0:T(4,128)S(1)}, f32[3,2,4,256]{3,2,1,0:T(4,128)S(1)}, u32[]{:S(2)}, u32[]{:S(2)}) collective-permute-start(f32[3,2,4,256]{3,2,1,0:T(4,128)S(1)} %get-tuple-element.29.sums0_ref), channel_id=1, source_target_pairs={{0,4},{4,0},{8,12},{12,8},{16,20},{20,16},{24,28},{28,24},{32,36},... | collective-permute-start | bytes 73736 | tf_op jit(solution)/shard_map/ppermute | solution.py:35
  31.1 0.7 collective-permute-start.9
  31.7 0.9 %collective-permute-done.8.from0_ref = f32[3,2,4,256]{3,2,1,0:T(4,128)S(1)} collective-permute-done((f32[3,2,4,256]{3,2,1,0:T(4,128)S(1)}, f32[3,2,4,256]{3,2,1,0:T(4,128)S(1)}, u32[]{:S(2)}, u32[]{:S(2)}) %collective-permute-start.8) | collective-permute-done | bytes 24608 | tf_op jit(solution)/shard_map/ppermute | solution.py:35
  32.6 0.0 collective-permute-done.9.from1_ref
  32.6 6.4 %chain_grads.1 = (f32[3,8,32,768]{3,2,1,0:T(8,128)}, bf16[3,4,32,768]{3,2,1,0:T(8,128)(2,1)S(1)}, bf16[3,4,32,768]{3,2,1,0:T(8,128)(2,1)S(1)}) custom-call(s32[128]{0:T(128)S(1)} %copy-done.5, s32[128]{0:T(128)S(1)} %copy-done.6, bf16[8,32,1536]{2,1,0:T(8,128)(2,1)S(1)} %copy-done, bf16[8,32,1536]{2,1,0:T(8,128)(2,1)S(1)} %copy-done.1, ...), custom_call_target="tpu_custom_call" | custom-call | tf_op jit(solution)/shard_map/chain_grads/pallas_call | solution.py:254
  39.0 5.2 %collective-permute-start.10 = (bf16[3,4,32,768]{3,2,1,0:T(8,128)(2,1)S(1)}, bf16[3,4,32,768]{3,2,1,0:T(8,128)(2,1)S(1)}, u32[]{:S(2)}, u32[]{:S(2)}) collective-permute-start(bf16[3,4,32,768]{3,2,1,0:T(8,128)(2,1)S(1)} %get-tuple-element.32), channel_id=1, source_target_pairs={{0,4},{4,0},{8,12},{12,8},{16,20},{20,16},{24,28},{28,24},{32,36},... | collective-permute-start | bytes 1769480 | tf_op jit(solution)/shard_map/ppermute | solution.py:35
  44.2 0.7 collective-permute-start.11
  44.9 0.0 collective-permute-done.in1_ref
  44.9 0.0 collective-permute-done.1.in2_ref
  44.9 1.1 %collective-permute-done.2.in3_ref = bf16[4,2,32,768]{3,2,1,0:T(8,128)(2,1)S(1)} collective-permute-done((bf16[4,2,32,768]{3,2,1,0:T(8,128)(2,1)S(1)}, bf16[4,2,32,768]{3,2,1,0:T(8,128)(2,1)S(1)}, u32[]{:S(2)}, u32[]{:S(2)}) %collective-permute-start.2) | collective-permute-done | bytes 393248 | tf_op jit(solution)/shard_map/ppermute | solution.py:40
  46.1 3.2 %space_grads.1 = (bf16[3,2,32,768]{3,2,1,0:T(8,128)(2,1)S(1)}, bf16[3,2,32,768]{3,2,1,0:T(8,128)(2,1)S(1)}, bf16[3,2,32,768]{3,2,1,0:T(8,128)(2,1)S(1)}, bf16[3,2,32,768]{3,2,1,0:T(8,128)(2,1)S(1)}) custom-call(bf16[8,32,1536]{2,1,0:T(8,128)(2,1)S(1)} %copy-done, bf16[8,32,1536]{2,1,0:T(8,128)(2,1)S(1)} %copy-done.1, bf16[8,32,1536]{2,1,0:T(8,128)(2,1)S(1)} %copy-done.2, ...), custom_call_target="tpu_custom_call" | custom-call | flops 400000000 | bytes 4000000 | tf_op jit(solution)/shard_map/space_grads/pallas_call | solution.py:311
  49.3 1.9 %collective-permute-start.3 = (bf16[3,2,32,768]{3,2,1,0:T(8,128)(2,1)S(1)}, bf16[3,2,32,768]{3,2,1,0:T(8,128)(2,1)S(1)}, u32[]{:S(2)}, u32[]{:S(2)}) collective-permute-start(bf16[3,2,32,768]{3,2,1,0:T(8,128)(2,1)S(1)} %get-tuple-element.24), channel_id=1, source_target_pairs={{0,1},{1,0},{2,3},{3,2},{4,5},{5,4},{6,7},{7,6},{8,9},{9,8},{10,11... | collective-permute-start | bytes 884744 | tf_op jit(solution)/shard_map/ppermute | solution.py:40
  51.2 2.8 %collective-permute-start.4 = (bf16[3,2,32,768]{3,2,1,0:T(8,128)(2,1)S(1)}, bf16[3,2,32,768]{3,2,1,0:T(8,128)(2,1)S(1)}, u32[]{:S(2)}, u32[]{:S(2)}) collective-permute-start(bf16[3,2,32,768]{3,2,1,0:T(8,128)(2,1)S(1)} %get-tuple-element.25), channel_id=1, source_target_pairs={{0,2},{1,3},{2,0},{3,1},{4,6},{5,7},{6,4},{7,5},{8,10},{9,11},{10,... | collective-permute-start | bytes 884744 | tf_op jit(solution)/shard_map/ppermute | solution.py:40
  54.0 0.5 collective-permute-start.5
  54.5 0.7 collective-permute-done.10.got0_ref
  55.1 0.0 collective-permute-done.11.got1_ref
  55.1 2.0 %finish_chain.1 = (bf16[8,32,1536]{2,1,0:T(8,128)(2,1)}, bf16[8,32,1536]{2,1,0:T(8,128)(2,1)}, bf16[8,32,1536]{2,1,0:T(8,128)(2,1)}) custom-call(s32[128]{0:T(128)S(1)} %copy-done.5, f32[3,8,32,768]{3,2,1,0:T(8,128)S(1)} %copy-done.4, bf16[3,4,32,768]{3,2,1,0:T(8,128)(2,1)S(1)} %collective-permute-done.10.got0_ref, ...), custom_call_target="tpu_custom_call" | custom-call | tf_op jit(solution)/shard_map/finish_chain/pallas_call | solution.py:339
  57.1 0.0 collective-permute-done.3.refs_1_
  57.1 17.0 %collective-permute-done.4.refs_2_ = bf16[3,2,32,768]{3,2,1,0:T(8,128)(2,1)S(1)} collective-permute-done((bf16[3,2,32,768]{3,2,1,0:T(8,128)(2,1)S(1)}, bf16[3,2,32,768]{3,2,1,0:T(8,128)(2,1)S(1)}, u32[]{:S(2)}, u32[]{:S(2)}) %collective-permute-start.4) | collective-permute-done | bytes 294944 | tf_op jit(solution)/shard_map/ppermute | solution.py:40
  74.1 6.3 %collective-permute-done.5.refs_3_ = bf16[3,2,32,768]{3,2,1,0:T(8,128)(2,1)S(1)} collective-permute-done((bf16[3,2,32,768]{3,2,1,0:T(8,128)(2,1)S(1)}, bf16[3,2,32,768]{3,2,1,0:T(8,128)(2,1)S(1)}, u32[]{:S(2)}, u32[]{:S(2)}) %collective-permute-start.5) | collective-permute-done | bytes 294944 | tf_op jit(solution)/shard_map/ppermute | solution.py:40
  80.5 1.2 %finish_space.1 = (bf16[8,32,1536]{2,1,0:T(8,128)(2,1)}, bf16[8,32,1536]{2,1,0:T(8,128)(2,1)}, bf16[8,32,1536]{2,1,0:T(8,128)(2,1)}) custom-call(bf16[3,2,32,768]{3,2,1,0:T(8,128)(2,1)S(1)} %get-tuple-element.23.refs_0_, bf16[3,2,32,768]{3,2,1,0:T(8,128)(2,1)S(1)} %collective-permute-done.3.refs_1_, ...), custom_call_target="tpu_custom_call", output_to_operand_aliasing={{0}: (4, {}), {1}: (5, {}), {2}: (6, {})} | custom-call | tf_op jit(solution)/shard_map/finish_space/pallas_call | solution.py:367
  (12 shorter events, 0.0 us)
Async XLA Ops:
  0.6 21.7 %copy-start.5 = (s32[128]{0:T(128)S(1)}, s32[128]{0:T(128)}, u32[]{:S(2)}) copy-start(s32[128]{0:T(128)} %order_ref.7) | copy-start | bytes 1540
  0.6 21.7 %copy-start.3 = (bf16[8,32,1536]{2,1,0:T(8,128)(2,1)S(1)}, bf16[8,32,1536]{2,1,0:T(8,128)(2,1)}, u32[]{:S(2)}) copy-start(bf16[8,32,1536]{2,1,0:T(8,128)(2,1)} %grad_ref.7) | copy-start | bytes 2359300
  0.7 21.7 %copy-start.2 = (bf16[8,32,1536]{2,1,0:T(8,128)(2,1)S(1)}, bf16[8,32,1536]{2,1,0:T(8,128)(2,1)}, u32[]{:S(2)}) copy-start(bf16[8,32,1536]{2,1,0:T(8,128)(2,1)} %value_ref.7) | copy-start | bytes 2359300
  0.7 21.7 %copy-start.1 = (bf16[8,32,1536]{2,1,0:T(8,128)(2,1)S(1)}, bf16[8,32,1536]{2,1,0:T(8,128)(2,1)}, u32[]{:S(2)}) copy-start(bf16[8,32,1536]{2,1,0:T(8,128)(2,1)} %key_ref.7) | copy-start | bytes 2359300
  0.7 21.7 %copy-start = (bf16[8,32,1536]{2,1,0:T(8,128)(2,1)S(1)}, bf16[8,32,1536]{2,1,0:T(8,128)(2,1)}, u32[]{:S(2)}) copy-start(bf16[8,32,1536]{2,1,0:T(8,128)(2,1)} %query_ref.7) | copy-start | bytes 2359300
  0.7 21.7 %copy-start.6 = (s32[128]{0:T(128)S(1)}, s32[128]{0:T(128)}, u32[]{:S(2)}) copy-start(s32[128]{0:T(128)} %lookback_ref.3) | copy-start | bytes 1540
  3.6 18.8 %collective-permute-start.6 = (bf16[4,4,32,768]{3,2,1,0:T(8,128)(2,1)S(1)}, bf16[4,4,32,768]{3,2,1,0:T(8,128)(2,1)S(1)}, u32[]{:S(2)}, u32[]{:S(2)}) collective-permute-start(bf16[4,4,32,768]{3,2,1,0:T(8,128)(2,1)S(1)} %get-tuple-element.27), channel_id=1, source_target_pairs={{0,4},{4,0},{8,12},{12,8},{16,20},{20,16},{24,28},{28,24},{32,36},... | collective-permute-start | bytes 2359304 | tf_op jit(solution)/shard_map/ppermute | solution.py:35
  6.1 16.2 %collective-permute-start.7 = (bf16[4,4,32,768]{3,2,1,0:T(8,128)(2,1)S(1)}, bf16[4,4,32,768]{3,2,1,0:T(8,128)(2,1)S(1)}, u32[]{:S(2)}, u32[]{:S(2)}) collective-permute-start(bf16[4,4,32,768]{3,2,1,0:T(8,128)(2,1)S(1)} %get-tuple-element.28), channel_id=1, source_target_pairs={{4,8},{8,4},{12,16},{16,12},{20,24},{24,20},{28,32},{32,28},{36,40... | collective-permute-start | bytes 2359304 | tf_op jit(solution)/shard_map/ppermute | solution.py:35
  6.8 38.0 %collective-permute-start = (bf16[4,2,32,768]{3,2,1,0:T(8,128)(2,1)S(1)}, bf16[4,2,32,768]{3,2,1,0:T(8,128)(2,1)S(1)}, u32[]{:S(2)}, u32[]{:S(2)}) collective-permute-start(bf16[4,2,32,768]{3,2,1,0:T(8,128)(2,1)S(1)} %get-tuple-element.20), channel_id=1, source_target_pairs={{0,1},{1,0},{2,3},{3,2},{4,5},{5,4},{6,7},{7,6},{8,9},{9,8},{10,11... | collective-permute-start | bytes 1179656 | tf_op jit(solution)/shard_map/ppermute | solution.py:40
  7.9 37.0 %collective-permute-start.1 = (bf16[4,2,32,768]{3,2,1,0:T(8,128)(2,1)S(1)}, bf16[4,2,32,768]{3,2,1,0:T(8,128)(2,1)S(1)}, u32[]{:S(2)}, u32[]{:S(2)}) collective-permute-start(bf16[4,2,32,768]{3,2,1,0:T(8,128)(2,1)S(1)} %get-tuple-element.21), channel_id=1, source_target_pairs={{0,2},{1,3},{2,0},{3,1},{4,6},{5,7},{6,4},{7,5},{8,10},{9,11},{10,... | collective-permute-start | bytes 1179656 | tf_op jit(solution)/shard_map/ppermute | solution.py:40
  10.7 35.4 %collective-permute-start.2 = (bf16[4,2,32,768]{3,2,1,0:T(8,128)(2,1)S(1)}, bf16[4,2,32,768]{3,2,1,0:T(8,128)(2,1)S(1)}, u32[]{:S(2)}, u32[]{:S(2)}) collective-permute-start(bf16[4,2,32,768]{3,2,1,0:T(8,128)(2,1)S(1)} %get-tuple-element.22), channel_id=1, source_target_pairs={{0,3},{1,2},{2,1},{3,0},{4,7},{5,6},{6,5},{7,4},{8,11},{9,10},{10,... | collective-permute-start | bytes 1179656 | tf_op jit(solution)/shard_map/ppermute | solution.py:40
  25.1 7.5 %collective-permute-start.8 = (f32[3,2,4,256]{3,2,1,0:T(4,128)S(1)}, f32[3,2,4,256]{3,2,1,0:T(4,128)S(1)}, u32[]{:S(2)}, u32[]{:S(2)}) collective-permute-start(f32[3,2,4,256]{3,2,1,0:T(4,128)S(1)} %get-tuple-element.29.sums0_ref), channel_id=1, source_target_pairs={{0,4},{4,0},{8,12},{12,8},{16,20},{20,16},{24,28},{28,24},{32,36},... | collective-permute-start | bytes 73736 | tf_op jit(solution)/shard_map/ppermute | solution.py:35
  31.1 1.5 %collective-permute-start.9 = (f32[3,2,4,256]{3,2,1,0:T(4,128)S(1)}, f32[3,2,4,256]{3,2,1,0:T(4,128)S(1)}, u32[]{:S(2)}, u32[]{:S(2)}) collective-permute-start(f32[3,2,4,256]{3,2,1,0:T(4,128)S(1)} %get-tuple-element.30.sums1_ref), channel_id=1, source_target_pairs={{4,8},{8,4},{12,16},{16,12},{20,24},{24,20},{28,32},{32,28},{36,40... | collective-permute-start | bytes 73736 | tf_op jit(solution)/shard_map/ppermute | solution.py:35
  39.0 16.1 %copy-start.4 = (f32[3,8,32,768]{3,2,1,0:T(8,128)S(1)}, f32[3,8,32,768]{3,2,1,0:T(8,128)}, u32[]{:S(2)}) copy-start(f32[3,8,32,768]{3,2,1,0:T(8,128)} %get-tuple-element.31.own_ref) | copy-start | bytes 7077892
  39.0 16.1 %collective-permute-start.10 = (bf16[3,4,32,768]{3,2,1,0:T(8,128)(2,1)S(1)}, bf16[3,4,32,768]{3,2,1,0:T(8,128)(2,1)S(1)}, u32[]{:S(2)}, u32[]{:S(2)}) collective-permute-start(bf16[3,4,32,768]{3,2,1,0:T(8,128)(2,1)S(1)} %get-tuple-element.32), channel_id=1, source_target_pairs={{0,4},{4,0},{8,12},{12,8},{16,20},{20,16},{24,28},{28,24},{32,36},... | collective-permute-start | bytes 1769480 | tf_op jit(solution)/shard_map/ppermute | solution.py:35
  44.2 10.9 %collective-permute-start.11 = (bf16[3,4,32,768]{3,2,1,0:T(8,128)(2,1)S(1)}, bf16[3,4,32,768]{3,2,1,0:T(8,128)(2,1)S(1)}, u32[]{:S(2)}, u32[]{:S(2)}) collective-permute-start(bf16[3,4,32,768]{3,2,1,0:T(8,128)(2,1)S(1)} %get-tuple-element.33), channel_id=1, source_target_pairs={{4,8},{8,4},{12,16},{16,12},{20,24},{24,20},{28,32},{32,28},{36,40... | collective-permute-start | bytes 1769480 | tf_op jit(solution)/shard_map/ppermute | solution.py:35
  49.3 7.8 %collective-permute-start.3 = (bf16[3,2,32,768]{3,2,1,0:T(8,128)(2,1)S(1)}, bf16[3,2,32,768]{3,2,1,0:T(8,128)(2,1)S(1)}, u32[]{:S(2)}, u32[]{:S(2)}) collective-permute-start(bf16[3,2,32,768]{3,2,1,0:T(8,128)(2,1)S(1)} %get-tuple-element.24), channel_id=1, source_target_pairs={{0,1},{1,0},{2,3},{3,2},{4,5},{5,4},{6,7},{7,6},{8,9},{9,8},{10,11... | collective-permute-start | bytes 884744 | tf_op jit(solution)/shard_map/ppermute | solution.py:40
  51.2 22.9 %collective-permute-start.4 = (bf16[3,2,32,768]{3,2,1,0:T(8,128)(2,1)S(1)}, bf16[3,2,32,768]{3,2,1,0:T(8,128)(2,1)S(1)}, u32[]{:S(2)}, u32[]{:S(2)}) collective-permute-start(bf16[3,2,32,768]{3,2,1,0:T(8,128)(2,1)S(1)} %get-tuple-element.25), channel_id=1, source_target_pairs={{0,2},{1,3},{2,0},{3,1},{4,6},{5,7},{6,4},{7,5},{8,10},{9,11},{10,... | collective-permute-start | bytes 884744 | tf_op jit(solution)/shard_map/ppermute | solution.py:40
  54.0 26.5 %collective-permute-start.5 = (bf16[3,2,32,768]{3,2,1,0:T(8,128)(2,1)S(1)}, bf16[3,2,32,768]{3,2,1,0:T(8,128)(2,1)S(1)}, u32[]{:S(2)}, u32[]{:S(2)}) collective-permute-start(bf16[3,2,32,768]{3,2,1,0:T(8,128)(2,1)S(1)} %get-tuple-element.26), channel_id=1, source_target_pairs={{0,3},{1,2},{2,1},{3,0},{4,7},{5,6},{6,5},{7,4},{8,11},{9,10},{10,... | collective-permute-start | bytes 884744 | tf_op jit(solution)/shard_map/ppermute | solution.py:40

commit v3 on v2

--- a/solution.py
+++ b/solution.py
@@ -55,46 +55,58 @@
     return jnp.where(odd == 1, device, late), jnp.where(odd == 1, late, device)
 
 
-def pack_kernel(order_ref, query_ref, key_ref, value_ref, grad_ref, *refs):
-    chain_refs, space_refs, sems = refs[:2], refs[2:5], refs[5]
+def pack_chain_kernel(order_ref, query_ref, key_ref, value_ref, grad_ref, out0_ref, out1_ref, sems):
     slot0, slot1 = side_slots(order_ref)
-    me = lax.axis_index("space")
     frames, _, width = key_ref.shape
-    half, share, columns = frames // 2, frames // 4, width // 2
+    half, columns = frames // 2, pl.ds(width // 2, width // 2)
     copies = []
-
-    def send(source, first, count, column, target):
-        piece = source.at[pl.ds(first, count), :, pl.ds(column, columns)]
-        copies.append(pltpu.make_async_copy(piece, target, sems.at[len(copies)]))
-
-    for here, there, out_ref in ((slot0, slot1, chain_refs[0]), (slot1, slot0, chain_refs[1])):
-        send(key_ref, there * half, half, columns, out_ref.at[0])
-        send(value_ref, there * half, half, columns, out_ref.at[1])
-        send(query_ref, here * half, half, columns, out_ref.at[2])
-        send(grad_ref, here * half, half, columns, out_ref.at[3])
-    for flip, out_ref in enumerate(space_refs, 1):
-        for part, source in enumerate((query_ref, key_ref, value_ref, grad_ref)):
-            send(source, (me ^ flip) * share, share, 0, out_ref.at[part])
+    for here, there, out_ref in ((slot0, slot1, out0_ref), (slot1, slot0, out1_ref)):
+        pieces = ((key_ref, there), (value_ref, there), (query_ref, here), (grad_ref, here))
+        for part, (source, slot) in enumerate(pieces):
+            piece = source.at[pl.ds(slot * half, half), :, columns]
+            copies.append(pltpu.make_async_copy(piece, out_ref.at[part], sems.at[len(copies)]))
     for copy in copies:
         copy.start()
     for copy in copies:
         copy.wait()
 
 
-def pack(group_order, query, key, value, grad):
-    frames, patches, width = key.shape
+def pack_space_kernel(*refs):
+    arrays, outs, sems = refs[:4], refs[4:7], refs[7]
+    me = lax.axis_index("space")
+    share, columns = outs[0].shape[1], pl.ds(0, outs[0].shape[3])
+    copies = []
+    for flip, out_ref in enumerate(outs, 1):
+        for part, source in enumerate(arrays):
+            piece = source.at[pl.ds((me ^ flip) * share, share), :, columns]
+            copies.append(pltpu.make_async_copy(piece, out_ref.at[part], sems.at[len(copies)]))
+    for copy in copies:
+        copy.start()
+    for copy in copies:
+        copy.wait()
+
+
+def pack(kernel, shapes, copies, scalars, arrays, name):
+    return pl.pallas_call(
+        kernel,
+        out_shape=shapes,
+        in_specs=[pl.BlockSpec(memory_space=pltpu.SMEM)] * len(scalars)
+        + [pl.BlockSpec(memory_space=pl.ANY)] * len(arrays),
+        out_specs=[pl.BlockSpec(memory_space=pl.ANY)] * len(shapes),
+        scratch_shapes=[pltpu.SemaphoreType.DMA((copies,))],
+        compiler_params=params(),
+        name=name,
+    )(*[pltpu.with_memory_space_constraint(x, pltpu.HBM) for x in (*scalars, *arrays)])
+
+
+def pack_all(group_order, *arrays):
+    frames, patches, width = arrays[0].shape
     chain = jax.ShapeDtypeStruct((4, frames // 2, patches, width // 2), BF16)
     space = jax.ShapeDtypeStruct((4, frames // 4, patches, width // 2), BF16)
-    outs = pl.pallas_call(
-        pack_kernel,
-        out_shape=(chain, chain, space, space, space),
-        in_specs=[pl.BlockSpec(memory_space=pltpu.SMEM)] + [pl.BlockSpec(memory_space=pl.ANY)] * 4,
-        out_specs=[pl.BlockSpec(memory_space=pl.ANY)] * 5,
-        scratch_shapes=[pltpu.SemaphoreType.DMA((20,))],
-        compiler_params=params(),
-        name="pack",
-    )(*[pltpu.with_memory_space_constraint(x, pltpu.HBM) for x in (group_order, query, key, value, grad)])
-    return outs[:2], outs[2:]
+    return (
+        pack(pack_chain_kernel, [chain] * 2, 8, (group_order,), arrays, "pack_chain"),
+        pack(pack_space_kernel, [space] * 3, 12, (), arrays, "pack_space"),
+    )
 
 
 def per_head(rows):
@@ -378,7 +390,7 @@
 
 
 def on_device(query, key, value, grad_out, group_order, lookback):
-    chain, sent = pack(group_order, query, key, value, grad_out)
+    chain, sent = pack_all(group_order, query, key, value, grad_out)
     arrived = [space_swap(part, flip) for flip, part in enumerate(sent, 1)]
     got = [chain_swap(part, phase) for phase, part in enumerate(chain)]
     ours = chain_sums(group_order, lookback, query, key, value, grad_out, *got)

time: 81.9 us -> 81.5 us (level)
  starting transfers between devices: 25.2 us -> 24.2 us
    ppermute x6, waiting for transfers between devices: 12.7 us -> 11.4 us  [chain_swap(): return lax.ppermute(value, 'tm', pairs)]
    ppermute x6, starting transfers between devices: 9.44 us -> 8.17 us  [space_swap(): return lax.ppermute(value, 'space', [(i, i ^ flip) for i in range(count)])]
    ppermute x6, waiting for transfers between devices: 24.5 us -> 25.6 us  [space_swap(): return lax.ppermute(value, 'space', [(i, i ^ flip) for i in range(count)])]
    pallas_call x1 -> x2, Pallas kernels: 2.89 us -> 3.66 us  [pack(): pl.pallas_call(kernel, out_shape=shapes, in_specs=[pl.BlockSpec(memory_sp...]
  transfers between devices with their start and end apart: 12 -> 12, of which waited for: 6 -> 6; matrix products, arithmetic and copies ran while one was open for 0% -> 0% of each run, Pallas kernels for 18% -> 19%
where the time goes in v3:
time: 81.5 us; the launch traced here: 81.3 us
  waiting for transfers between devices  37.1 us (46%)
  starting transfers between devices  24.2 us (30%)
  Pallas kernels  19.2 us (24%)
    ppermute x6, waiting for transfers between devices, space_swap(): return lax.ppermute(value, 'space', [(i, i ^ flip) for i in range(count)])  25.6 us
    ppermute x6, starting transfers between devices, chain_swap(): return lax.ppermute(value, 'tm', pairs)  16 us
    ppermute x6, waiting for transfers between devices, chain_swap(): return lax.ppermute(value, 'tm', pairs)  11.4 us
    pallas_call x2, Pallas kernels, chain_call(): pl.pallas_call(kernel, in_specs=[pl.BlockSpec(memory_space=pltpu.SMEM)] *...  9.11 us
    ppermute x6, starting transfers between devices, space_swap(): return lax.ppermute(value, 'space', [(i, i ^ flip) for i in range(count)])  8.17 us
    pallas_call x2, Pallas kernels, pack(): pl.pallas_call(kernel, out_shape=shapes, in_specs=[pl.BlockSpec(memory_sp...  3.66 us
    pallas_call x1, Pallas kernels, space_grads(): pl.pallas_call(space_kernel, grid=(columns // SPACE_LANES,), in_specs=[ow...  3.24 us
    pallas_call x1, Pallas kernels, finish_chain(): pl.pallas_call(finish_chain_kernel, grid_spec=pltpu.PrefetchScalarGridSpe...  1.96 us
  transfers between devices with their start and end apart: 12, of which 6 were waited for; matrix products, arithmetic and copies ran while one was open for 0% of the time, Pallas kernels for 19%

profile of v3, /device:TPU:1, one launch (start us, length us, event | category | flops | bytes accessed | tf_op | source)
XLA Modules:
  0.0 81.3 jit_solution(3102252139304845699)
XLA Ops:
  0.6 2.2 %pack_chain.1 = (bf16[4,4,32,768]{3,2,1,0:T(8,128)(2,1)S(1)}, bf16[4,4,32,768]{3,2,1,0:T(8,128)(2,1)S(1)}) custom-call(s32[128]{0:T(128)} %order_ref.7, bf16[8,32,1536]{2,1,0:T(8,128)(2,1)} %query_ref.7, bf16[8,32,1536]{2,1,0:T(8,128)(2,1)} %key_ref.7, bf16[8,32,1536]{2,1,0:T(8,128)(2,1)} %value_ref.7, bf16[8,32,1536]{2,1,0:T(8,128)(2,1)} %grad_ref.7), custom_call_target="tpu_custom_call" | custom-call | tf_op jit(solution)/shard_map/pack_chain/pallas_call | solution.py:90
  2.8 0.0 copy-start
  2.9 0.0 copy-start.1
  2.9 0.0 copy-start.2
  2.9 0.0 copy-start.3
  2.9 0.0 copy-start.5
  2.9 0.0 copy-start.6
  2.9 2.6 %collective-permute-start.6 = (bf16[4,4,32,768]{3,2,1,0:T(8,128)(2,1)S(1)}, bf16[4,4,32,768]{3,2,1,0:T(8,128)(2,1)S(1)}, u32[]{:S(2)}, u32[]{:S(2)}) collective-permute-start(bf16[4,4,32,768]{3,2,1,0:T(8,128)(2,1)S(1)} %get-tuple-element.27), channel_id=1, source_target_pairs={{0,4},{4,0},{8,12},{12,8},{16,20},{20,16},{24,28},{28,24},{32,36},... | collective-permute-start | bytes 2359304 | tf_op jit(solution)/shard_map/ppermute | solution.py:35
  5.5 0.7 collective-permute-start.7
  6.2 1.4 %pack_space.1 = (bf16[4,2,32,768]{3,2,1,0:T(8,128)(2,1)S(1)}, bf16[4,2,32,768]{3,2,1,0:T(8,128)(2,1)S(1)}, bf16[4,2,32,768]{3,2,1,0:T(8,128)(2,1)S(1)}) custom-call(bf16[8,32,1536]{2,1,0:T(8,128)(2,1)} %query_ref.7, bf16[8,32,1536]{2,1,0:T(8,128)(2,1)} %key_ref.7, bf16[8,32,1536]{2,1,0:T(8,128)(2,1)} %value_ref.7, bf16[8,32,1536]{2,1,0:T(8,128)(2,1)} %grad_ref.7), custom_call_target="tpu_custom_call" | custom-call | tf_op jit(solution)/shard_map/pack_space/pallas_call | solution.py:90
  7.6 1.2 %collective-permute-start = (bf16[4,2,32,768]{3,2,1,0:T(8,128)(2,1)S(1)}, bf16[4,2,32,768]{3,2,1,0:T(8,128)(2,1)S(1)}, u32[]{:S(2)}, u32[]{:S(2)}) collective-permute-start(bf16[4,2,32,768]{3,2,1,0:T(8,128)(2,1)S(1)} %get-tuple-element.20), channel_id=1, source_target_pairs={{0,1},{1,0},{2,3},{3,2},{4,5},{5,4},{6,7},{7,6},{8,9},{9,8},{10,11... | collective-permute-start | bytes 1179656 | tf_op jit(solution)/shard_map/ppermute | solution.py:40
  8.8 2.6 %collective-permute-start.1 = (bf16[4,2,32,768]{3,2,1,0:T(8,128)(2,1)S(1)}, bf16[4,2,32,768]{3,2,1,0:T(8,128)(2,1)S(1)}, u32[]{:S(2)}, u32[]{:S(2)}) collective-permute-start(bf16[4,2,32,768]{3,2,1,0:T(8,128)(2,1)S(1)} %get-tuple-element.21), channel_id=1, source_target_pairs={{0,2},{1,3},{2,0},{3,1},{4,6},{5,7},{6,4},{7,5},{8,10},{9,11},{10,... | collective-permute-start | bytes 1179656 | tf_op jit(solution)/shard_map/ppermute | solution.py:40
  11.4 0.6 collective-permute-start.2
  12.0 9.6 %collective-permute-done.6.got0_ref = bf16[4,4,32,768]{3,2,1,0:T(8,128)(2,1)S(1)} collective-permute-done((bf16[4,4,32,768]{3,2,1,0:T(8,128)(2,1)S(1)}, bf16[4,4,32,768]{3,2,1,0:T(8,128)(2,1)S(1)}, u32[]{:S(2)}, u32[]{:S(2)}) %collective-permute-start.6) | collective-permute-done | bytes 786464 | tf_op jit(solution)/shard_map/ppermute | solution.py:35
  21.7 0.0 collective-permute-done.7.got1_ref
  21.7 2.7 %chain_sums.1 = (f32[3,2,4,256]{3,2,1,0:T(4,128)S(1)}, f32[3,2,4,256]{3,2,1,0:T(4,128)S(1)}) custom-call(s32[128]{0:T(128)S(1)} %copy-done.5, s32[128]{0:T(128)S(1)} %copy-done.6, bf16[8,32,1536]{2,1,0:T(8,128)(2,1)S(1)} %copy-done, bf16[8,32,1536]{2,1,0:T(8,128)(2,1)S(1)} %copy-done.1, bf16[8,32,1536]{2,1,0:T(8,128)(2,1)S(1)} %copy-done.2, ...), custom_call_target="tpu_custom_call" | custom-call | tf_op jit(solution)/shard_map/chain_sums/pallas_call | solution.py:266
  24.4 6.0 %collective-permute-start.8 = (f32[3,2,4,256]{3,2,1,0:T(4,128)S(1)}, f32[3,2,4,256]{3,2,1,0:T(4,128)S(1)}, u32[]{:S(2)}, u32[]{:S(2)}) collective-permute-start(f32[3,2,4,256]{3,2,1,0:T(4,128)S(1)} %get-tuple-element.29.sums0_ref), channel_id=1, source_target_pairs={{0,4},{4,0},{8,12},{12,8},{16,20},{20,16},{24,28},{28,24},{32,36},... | collective-permute-start | bytes 73736 | tf_op jit(solution)/shard_map/ppermute | solution.py:35
  30.4 0.7 collective-permute-start.9
  31.1 0.9 %collective-permute-done.8.from0_ref = f32[3,2,4,256]{3,2,1,0:T(4,128)S(1)} collective-permute-done((f32[3,2,4,256]{3,2,1,0:T(4,128)S(1)}, f32[3,2,4,256]{3,2,1,0:T(4,128)S(1)}, u32[]{:S(2)}, u32[]{:S(2)}) %collective-permute-start.8) | collective-permute-done | bytes 24608 | tf_op jit(solution)/shard_map/ppermute | solution.py:35
  31.9 6.4 %chain_grads.1 = (f32[3,8,32,768]{3,2,1,0:T(8,128)}, bf16[3,4,32,768]{3,2,1,0:T(8,128)(2,1)S(1)}, bf16[3,4,32,768]{3,2,1,0:T(8,128)(2,1)S(1)}) custom-call(s32[128]{0:T(128)S(1)} %copy-done.5, s32[128]{0:T(128)S(1)} %copy-done.6, bf16[8,32,1536]{2,1,0:T(8,128)(2,1)S(1)} %copy-done, bf16[8,32,1536]{2,1,0:T(8,128)(2,1)S(1)} %copy-done.1, ...), custom_call_target="tpu_custom_call" | custom-call | tf_op jit(solution)/shard_map/chain_grads/pallas_call | solution.py:266
  38.3 5.5 %collective-permute-start.10 = (bf16[3,4,32,768]{3,2,1,0:T(8,128)(2,1)S(1)}, bf16[3,4,32,768]{3,2,1,0:T(8,128)(2,1)S(1)}, u32[]{:S(2)}, u32[]{:S(2)}) collective-permute-start(bf16[3,4,32,768]{3,2,1,0:T(8,128)(2,1)S(1)} %get-tuple-element.32), channel_id=1, source_target_pairs={{0,4},{4,0},{8,12},{12,8},{16,20},{20,16},{24,28},{28,24},{32,36},... | collective-permute-start | bytes 1769480 | tf_op jit(solution)/shard_map/ppermute | solution.py:35
  43.8 0.7 collective-permute-start.11
  44.5 2.5 %collective-permute-done.2.in3_ref = bf16[4,2,32,768]{3,2,1,0:T(8,128)(2,1)S(1)} collective-permute-done((bf16[4,2,32,768]{3,2,1,0:T(8,128)(2,1)S(1)}, bf16[4,2,32,768]{3,2,1,0:T(8,128)(2,1)S(1)}, u32[]{:S(2)}, u32[]{:S(2)}) %collective-permute-start.2) | collective-permute-done | bytes 393248 | tf_op jit(solution)/shard_map/ppermute | solution.py:40
  47.0 3.2 %space_grads.1 = (bf16[3,2,32,768]{3,2,1,0:T(8,128)(2,1)S(1)}, bf16[3,2,32,768]{3,2,1,0:T(8,128)(2,1)S(1)}, bf16[3,2,32,768]{3,2,1,0:T(8,128)(2,1)S(1)}, bf16[3,2,32,768]{3,2,1,0:T(8,128)(2,1)S(1)}) custom-call(bf16[8,32,1536]{2,1,0:T(8,128)(2,1)S(1)} %copy-done, bf16[8,32,1536]{2,1,0:T(8,128)(2,1)S(1)} %copy-done.1, bf16[8,32,1536]{2,1,0:T(8,128)(2,1)S(1)} %copy-done.2, ...), custom_call_target="tpu_custom_call" | custom-call | flops 400000000 | bytes 4000000 | tf_op jit(solution)/shard_map/space_grads/pallas_call | solution.py:323
  50.2 0.5 collective-permute-start.3
  50.7 2.8 %collective-permute-start.4 = (bf16[3,2,32,768]{3,2,1,0:T(8,128)(2,1)S(1)}, bf16[3,2,32,768]{3,2,1,0:T(8,128)(2,1)S(1)}, u32[]{:S(2)}, u32[]{:S(2)}) collective-permute-start(bf16[3,2,32,768]{3,2,1,0:T(8,128)(2,1)S(1)} %get-tuple-element.25), channel_id=1, source_target_pairs={{0,2},{1,3},{2,0},{3,1},{4,6},{5,7},{6,4},{7,5},{8,10},{9,11},{10,... | collective-permute-start | bytes 884744 | tf_op jit(solution)/shard_map/ppermute | solution.py:40
  53.5 0.5 collective-permute-start.5
  54.0 0.9 %collective-permute-done.10.got0_ref = bf16[3,4,32,768]{3,2,1,0:T(8,128)(2,1)S(1)} collective-permute-done((bf16[3,4,32,768]{3,2,1,0:T(8,128)(2,1)S(1)}, bf16[3,4,32,768]{3,2,1,0:T(8,128)(2,1)S(1)}, u32[]{:S(2)}, u32[]{:S(2)}) %collective-permute-start.10) | collective-permute-done | bytes 589856 | tf_op jit(solution)/shard_map/ppermute | solution.py:35
  54.9 2.0 %finish_chain.1 = (bf16[8,32,1536]{2,1,0:T(8,128)(2,1)}, bf16[8,32,1536]{2,1,0:T(8,128)(2,1)}, bf16[8,32,1536]{2,1,0:T(8,128)(2,1)}) custom-call(s32[128]{0:T(128)S(1)} %copy-done.5, f32[3,8,32,768]{3,2,1,0:T(8,128)S(1)} %copy-done.4, bf16[3,4,32,768]{3,2,1,0:T(8,128)(2,1)S(1)} %collective-permute-done.10.got0_ref, ...), custom_call_target="tpu_custom_call" | custom-call | tf_op jit(solution)/shard_map/finish_chain/pallas_call | solution.py:351
  56.9 16.9 %collective-permute-done.4.refs_2_ = bf16[3,2,32,768]{3,2,1,0:T(8,128)(2,1)S(1)} collective-permute-done((bf16[3,2,32,768]{3,2,1,0:T(8,128)(2,1)S(1)}, bf16[3,2,32,768]{3,2,1,0:T(8,128)(2,1)S(1)}, u32[]{:S(2)}, u32[]{:S(2)}) %collective-permute-start.4) | collective-permute-done | bytes 294944 | tf_op jit(solution)/shard_map/ppermute | solution.py:40
  73.7 6.3 %collective-permute-done.5.refs_3_ = bf16[3,2,32,768]{3,2,1,0:T(8,128)(2,1)S(1)} collective-permute-done((bf16[3,2,32,768]{3,2,1,0:T(8,128)(2,1)S(1)}, bf16[3,2,32,768]{3,2,1,0:T(8,128)(2,1)S(1)}, u32[]{:S(2)}, u32[]{:S(2)}) %collective-permute-start.5) | collective-permute-done | bytes 294944 | tf_op jit(solution)/shard_map/ppermute | solution.py:40
  80.1 1.2 %finish_space.1 = (bf16[8,32,1536]{2,1,0:T(8,128)(2,1)}, bf16[8,32,1536]{2,1,0:T(8,128)(2,1)}, bf16[8,32,1536]{2,1,0:T(8,128)(2,1)}) custom-call(bf16[3,2,32,768]{3,2,1,0:T(8,128)(2,1)S(1)} %get-tuple-element.23.refs_0_, bf16[3,2,32,768]{3,2,1,0:T(8,128)(2,1)S(1)} %collective-permute-done.3.refs_1_, ...), custom_call_target="tpu_custom_call", output_to_operand_aliasing={{0}: (4, {}), {1}: (5, {}), {2}: (6, {})} | custom-call | tf_op jit(solution)/shard_map/finish_space/pallas_call | solution.py:379
  (13 shorter events, 0.0 us)
Async XLA Ops:
  2.8 18.8 %copy-start = (bf16[8,32,1536]{2,1,0:T(8,128)(2,1)S(1)}, bf16[8,32,1536]{2,1,0:T(8,128)(2,1)}, u32[]{:S(2)}) copy-start(bf16[8,32,1536]{2,1,0:T(8,128)(2,1)} %query_ref.7) | copy-start | bytes 2359300
  2.9 18.8 %copy-start.1 = (bf16[8,32,1536]{2,1,0:T(8,128)(2,1)S(1)}, bf16[8,32,1536]{2,1,0:T(8,128)(2,1)}, u32[]{:S(2)}) copy-start(bf16[8,32,1536]{2,1,0:T(8,128)(2,1)} %key_ref.7) | copy-start | bytes 2359300
  2.9 18.8 %copy-start.2 = (bf16[8,32,1536]{2,1,0:T(8,128)(2,1)S(1)}, bf16[8,32,1536]{2,1,0:T(8,128)(2,1)}, u32[]{:S(2)}) copy-start(bf16[8,32,1536]{2,1,0:T(8,128)(2,1)} %value_ref.7) | copy-start | bytes 2359300
  2.9 18.8 %copy-start.3 = (bf16[8,32,1536]{2,1,0:T(8,128)(2,1)S(1)}, bf16[8,32,1536]{2,1,0:T(8,128)(2,1)}, u32[]{:S(2)}) copy-start(bf16[8,32,1536]{2,1,0:T(8,128)(2,1)} %grad_ref.7) | copy-start | bytes 2359300
  2.9 18.8 %copy-start.5 = (s32[128]{0:T(128)S(1)}, s32[128]{0:T(128)}, u32[]{:S(2)}) copy-start(s32[128]{0:T(128)} %order_ref.7) | copy-start | bytes 1540
  2.9 18.8 %copy-start.6 = (s32[128]{0:T(128)S(1)}, s32[128]{0:T(128)}, u32[]{:S(2)}) copy-start(s32[128]{0:T(128)} %lookback_ref.3) | copy-start | bytes 1540
  2.9 18.8 %collective-permute-start.6 = (bf16[4,4,32,768]{3,2,1,0:T(8,128)(2,1)S(1)}, bf16[4,4,32,768]{3,2,1,0:T(8,128)(2,1)S(1)}, u32[]{:S(2)}, u32[]{:S(2)}) collective-permute-start(bf16[4,4,32,768]{3,2,1,0:T(8,128)(2,1)S(1)} %get-tuple-element.27), channel_id=1, source_target_pairs={{0,4},{4,0},{8,12},{12,8},{16,20},{20,16},{24,28},{28,24},{32,36},... | collective-permute-start | bytes 2359304 | tf_op jit(solution)/shard_map/ppermute | solution.py:35
  5.5 16.2 %collective-permute-start.7 = (bf16[4,4,32,768]{3,2,1,0:T(8,128)(2,1)S(1)}, bf16[4,4,32,768]{3,2,1,0:T(8,128)(2,1)S(1)}, u32[]{:S(2)}, u32[]{:S(2)}) collective-permute-start(bf16[4,4,32,768]{3,2,1,0:T(8,128)(2,1)S(1)} %get-tuple-element.28), channel_id=1, source_target_pairs={{4,8},{8,4},{12,16},{16,12},{20,24},{24,20},{28,32},{32,28},{36,40... | collective-permute-start | bytes 2359304 | tf_op jit(solution)/shard_map/ppermute | solution.py:35
  7.6 36.9 %collective-permute-start = (bf16[4,2,32,768]{3,2,1,0:T(8,128)(2,1)S(1)}, bf16[4,2,32,768]{3,2,1,0:T(8,128)(2,1)S(1)}, u32[]{:S(2)}, u32[]{:S(2)}) collective-permute-start(bf16[4,2,32,768]{3,2,1,0:T(8,128)(2,1)S(1)} %get-tuple-element.20), channel_id=1, source_target_pairs={{0,1},{1,0},{2,3},{3,2},{4,5},{5,4},{6,7},{7,6},{8,9},{9,8},{10,11... | collective-permute-start | bytes 1179656 | tf_op jit(solution)/shard_map/ppermute | solution.py:40
  8.8 35.7 %collective-permute-start.1 = (bf16[4,2,32,768]{3,2,1,0:T(8,128)(2,1)S(1)}, bf16[4,2,32,768]{3,2,1,0:T(8,128)(2,1)S(1)}, u32[]{:S(2)}, u32[]{:S(2)}) collective-permute-start(bf16[4,2,32,768]{3,2,1,0:T(8,128)(2,1)S(1)} %get-tuple-element.21), channel_id=1, source_target_pairs={{0,2},{1,3},{2,0},{3,1},{4,6},{5,7},{6,4},{7,5},{8,10},{9,11},{10,... | collective-permute-start | bytes 1179656 | tf_op jit(solution)/shard_map/ppermute | solution.py:40
  11.4 35.5 %collective-permute-start.2 = (bf16[4,2,32,768]{3,2,1,0:T(8,128)(2,1)S(1)}, bf16[4,2,32,768]{3,2,1,0:T(8,128)(2,1)S(1)}, u32[]{:S(2)}, u32[]{:S(2)}) collective-permute-start(bf16[4,2,32,768]{3,2,1,0:T(8,128)(2,1)S(1)} %get-tuple-element.22), channel_id=1, source_target_pairs={{0,3},{1,2},{2,1},{3,0},{4,7},{5,6},{6,5},{7,4},{8,11},{9,10},{10,... | collective-permute-start | bytes 1179656 | tf_op jit(solution)/shard_map/ppermute | solution.py:40
  24.4 7.5 %collective-permute-start.8 = (f32[3,2,4,256]{3,2,1,0:T(4,128)S(1)}, f32[3,2,4,256]{3,2,1,0:T(4,128)S(1)}, u32[]{:S(2)}, u32[]{:S(2)}) collective-permute-start(f32[3,2,4,256]{3,2,1,0:T(4,128)S(1)} %get-tuple-element.29.sums0_ref), channel_id=1, source_target_pairs={{0,4},{4,0},{8,12},{12,8},{16,20},{20,16},{24,28},{28,24},{32,36},... | collective-permute-start | bytes 73736 | tf_op jit(solution)/shard_map/ppermute | solution.py:35
  30.4 1.5 %collective-permute-start.9 = (f32[3,2,4,256]{3,2,1,0:T(4,128)S(1)}, f32[3,2,4,256]{3,2,1,0:T(4,128)S(1)}, u32[]{:S(2)}, u32[]{:S(2)}) collective-permute-start(f32[3,2,4,256]{3,2,1,0:T(4,128)S(1)} %get-tuple-element.30.sums1_ref), channel_id=1, source_target_pairs={{4,8},{8,4},{12,16},{16,12},{20,24},{24,20},{28,32},{32,28},{36,40... | collective-permute-start | bytes 73736 | tf_op jit(solution)/shard_map/ppermute | solution.py:35
  38.3 16.6 %copy-start.4 = (f32[3,8,32,768]{3,2,1,0:T(8,128)S(1)}, f32[3,8,32,768]{3,2,1,0:T(8,128)}, u32[]{:S(2)}) copy-start(f32[3,8,32,768]{3,2,1,0:T(8,128)} %get-tuple-element.31.own_ref) | copy-start | bytes 7077892
  38.3 16.6 %collective-permute-start.10 = (bf16[3,4,32,768]{3,2,1,0:T(8,128)(2,1)S(1)}, bf16[3,4,32,768]{3,2,1,0:T(8,128)(2,1)S(1)}, u32[]{:S(2)}, u32[]{:S(2)}) collective-permute-start(bf16[3,4,32,768]{3,2,1,0:T(8,128)(2,1)S(1)} %get-tuple-element.32), channel_id=1, source_target_pairs={{0,4},{4,0},{8,12},{12,8},{16,20},{20,16},{24,28},{28,24},{32,36},... | collective-permute-start | bytes 1769480 | tf_op jit(solution)/shard_map/ppermute | solution.py:35
  43.8 11.1 %collective-permute-start.11 = (bf16[3,4,32,768]{3,2,1,0:T(8,128)(2,1)S(1)}, bf16[3,4,32,768]{3,2,1,0:T(8,128)(2,1)S(1)}, u32[]{:S(2)}, u32[]{:S(2)}) collective-permute-start(bf16[3,4,32,768]{3,2,1,0:T(8,128)(2,1)S(1)} %get-tuple-element.33), channel_id=1, source_target_pairs={{4,8},{8,4},{12,16},{16,12},{20,24},{24,20},{28,32},{32,28},{36,40... | collective-permute-start | bytes 1769480 | tf_op jit(solution)/shard_map/ppermute | solution.py:35
  50.2 6.6 %collective-permute-start.3 = (bf16[3,2,32,768]{3,2,1,0:T(8,128)(2,1)S(1)}, bf16[3,2,32,768]{3,2,1,0:T(8,128)(2,1)S(1)}, u32[]{:S(2)}, u32[]{:S(2)}) collective-permute-start(bf16[3,2,32,768]{3,2,1,0:T(8,128)(2,1)S(1)} %get-tuple-element.24), channel_id=1, source_target_pairs={{0,1},{1,0},{2,3},{3,2},{4,5},{5,4},{6,7},{7,6},{8,9},{9,8},{10,11... | collective-permute-start | bytes 884744 | tf_op jit(solution)/shard_map/ppermute | solution.py:40
  50.7 23.0 %collective-permute-start.4 = (bf16[3,2,32,768]{3,2,1,0:T(8,128)(2,1)S(1)}, bf16[3,2,32,768]{3,2,1,0:T(8,128)(2,1)S(1)}, u32[]{:S(2)}, u32[]{:S(2)}) collective-permute-start(bf16[3,2,32,768]{3,2,1,0:T(8,128)(2,1)S(1)} %get-tuple-element.25), channel_id=1, source_target_pairs={{0,2},{1,3},{2,0},{3,1},{4,6},{5,7},{6,4},{7,5},{8,10},{9,11},{10,... | collective-permute-start | bytes 884744 | tf_op jit(solution)/shard_map/ppermute | solution.py:40
  53.5 26.6 %collective-permute-start.5 = (bf16[3,2,32,768]{3,2,1,0:T(8,128)(2,1)S(1)}, bf16[3,2,32,768]{3,2,1,0:T(8,128)(2,1)S(1)}, u32[]{:S(2)}, u32[]{:S(2)}) collective-permute-start(bf16[3,2,32,768]{3,2,1,0:T(8,128)(2,1)S(1)} %get-tuple-element.26), channel_id=1, source_target_pairs={{0,3},{1,2},{2,1},{3,0},{4,7},{5,6},{6,5},{7,4},{8,11},{9,10},{10,... | collective-permute-start | bytes 884744 | tf_op jit(solution)/shard_map/ppermute | solution.py:40
